TPU v7x, 128 devices: a whole 4x4x4 slice. The times are simulated.
128 devices in a mesh: seq: 16 (over z_hi, y, core), dp: 8 (over z_lo, x).
Axes of the slice: x: 4, y: 4, z: 4 (z_hi: 2, z_lo: 2; z = z_hi * 2 + z_lo), core: 2. Of those that a mesh axis runs over, the one named last changes fastest.
Arguments:
- queries: bfloat16 [8, 4096, 2048], P('dp', 'seq'), may hold values from -34 to 34
- key_heads: bfloat16 [8, 4096, 512], P('dp', 'seq'), may hold values from -7 to 7
- value_heads: bfloat16 [8, 4096, 512], P('dp', 'seq'), may hold values from -6 to 6
- doc_lengths: int32 [8, 32], P('dp'), may hold values from 1 to 256, 4096 in all within a row
- out_weight: bfloat16 [2048, 2048], P('dp'), may hold values from -0.125 to 0.125
- cotangent: bfloat16 [8, 4096, 2048], P('dp', 'seq'), may hold values from -6 to 6
Outputs:
- projected: bfloat16 [8, 4096, 2048], P('dp', 'seq')
- grad_queries: bfloat16 [8, 4096, 2048], P('dp', 'seq')
- grad_keys: bfloat16 [8, 4096, 512], P('dp', 'seq')
- grad_values: bfloat16 [8, 4096, 512], P('dp', 'seq')
- grad_weight: float32 [2048, 2048], P('dp')
Inputs may be any that keep to these rules, and one draw needn't show every extreme that they name: `doc_lengths`: each pack's documents lie end to end in this order and fill its 4096 tokens; no document is longer than 256 tokens, and in every pack one document is exactly that long.
All inputs are finite; a program needn't handle non-finite values.
Results may differ from a plain program's by a relative error of at most 0.017.
Values may be sent and summed in bfloat16 or wider, within the bound.
A program may use at most 128 MiB of HBM per device.

v0:
```python
import math

import jax
import jax.numpy as jnp
from jax import lax
from jax.sharding import PartitionSpec as P

HQ = 16
HK = 4
DH = 128
DM = 2048


def from_behind(value, axis, by):
    devices = lax.axis_size(axis)
    pairs = [(i, i + by) for i in range(devices) if 0 <= i + by < devices]
    return lax.ppermute(value, axis, pairs)


def shortened(value):
    return jax.tree.map(lambda a: a.astype(jnp.bfloat16) if a.dtype == jnp.float32 else a, value)


def doc_begin(lengths, position):
    ending = jnp.cumsum(lengths)
    opening = ending - lengths
    covered = opening[None, :] <= position[:, None]
    return jnp.max(jnp.where(covered, opening[None, :], 0), axis=-1)


def attend_local(query, key_block, value_block, grad_att, q_begin, q_pos, k_pos):
    rows = query.shape[0]
    group = HQ // HK
    scale = 1.0 / math.sqrt(DH)
    allowed = (k_pos[None, :] >= q_begin[:, None]) & (k_pos[None, :] <= q_pos[:, None])
    attended_parts, query_parts, key_parts, value_parts = ([], [], [], [])
    for kv_group in range(HK):
        low_q = kv_group * group * DH
        high_q = (kv_group + 1) * group * DH
        q_part = query[:, low_q:high_q].reshape(rows, group, DH)
        g_part = grad_att[:, low_q:high_q].reshape(rows, group, DH)
        k_part = key_block[:, kv_group * DH : (kv_group + 1) * DH]
        v_part = value_block[:, kv_group * DH : (kv_group + 1) * DH]
        scores = (
            jnp.einsum("igd,jd->gij", q_part, k_part, preferred_element_type=jnp.float32) * scale
        )
        scores = jnp.where(allowed[None], scores, -jnp.inf)
        peak = jnp.max(scores, axis=-1, keepdims=True)
        logsum = peak + jnp.log(jnp.sum(jnp.exp(scores - peak), axis=-1, keepdims=True))
        probs = jnp.exp(scores - logsum)
        probs_low = probs.astype(jnp.bfloat16)
        attended = jnp.einsum(
            "gij,jd->igd", probs_low, v_part, preferred_element_type=jnp.float32
        ).astype(jnp.bfloat16)
        delta = jnp.einsum("igd,igd->gi", g_part, attended, preferred_element_type=jnp.float32)
        grad_probs = jnp.einsum("igd,jd->gij", g_part, v_part, preferred_element_type=jnp.float32)
        grad_low = (probs * (grad_probs - delta[:, :, None])).astype(jnp.bfloat16)
        grad_query = (
            jnp.einsum("gij,jd->igd", grad_low, k_part, preferred_element_type=jnp.float32) * scale
        ).astype(jnp.bfloat16)
        grad_key = (
            jnp.einsum("gij,igd->jd", grad_low, q_part, preferred_element_type=jnp.float32) * scale
        )
        grad_value = jnp.einsum(
            "gij,igd->jd", probs_low, g_part, preferred_element_type=jnp.float32
        )
        attended_parts.append(attended.reshape(rows, group * DH))
        query_parts.append(grad_query.reshape(rows, group * DH))
        key_parts.append(grad_key)
        value_parts.append(grad_value)
    return (
        jnp.concatenate(attended_parts, axis=-1),
        jnp.concatenate(query_parts, axis=-1),
        jnp.concatenate(key_parts, axis=-1),
        jnp.concatenate(value_parts, axis=-1),
    )


def body(queries, key_heads, value_heads, doc_lengths, out_weight, cotangent):
    packs_here, rows, width_q = queries.shape
    seq_count = lax.axis_size("seq")
    dp_count = lax.axis_size("dp")
    first = lax.axis_index("seq") * rows
    q_pos = first + jnp.arange(rows, dtype=jnp.int32)
    k_pos = first - rows + jnp.arange(2 * rows, dtype=jnp.int32)

    def pack_begin(lengths):
        return doc_begin(lengths, q_pos)

    begins = jax.vmap(pack_begin)(doc_lengths)
    earlier_keys, earlier_values = from_behind((key_heads, value_heads), "seq", 1)
    key_block = jnp.concatenate([earlier_keys, key_heads], axis=1)
    value_block = jnp.concatenate([earlier_values, value_heads], axis=1)
    flat_cot = cotangent.reshape(packs_here * rows, DM)
    full_weight = lax.all_gather(out_weight, "dp", axis=0, tiled=True)
    grad_att = jnp.einsum(
        "td,qd->tq", flat_cot, full_weight, preferred_element_type=jnp.float32
    ).astype(jnp.bfloat16)
    grad_att = grad_att.reshape(packs_here, rows, width_q)

    def per_pack(query, keys_here, values_here, grad_here, begin_here):
        return attend_local(query, keys_here, values_here, grad_here, begin_here, q_pos, k_pos)

    attended, grad_queries, grad_key_block, grad_value_block = jax.vmap(per_pack)(
        queries, key_block, value_block, grad_att, begins
    )
    returned_keys, returned_values = from_behind(
        (shortened(grad_key_block[:, :rows]), shortened(grad_value_block[:, :rows])), "seq", -1
    )
    grad_keys = (grad_key_block[:, rows:] + returned_keys).astype(jnp.bfloat16)
    grad_values = (grad_value_block[:, rows:] + returned_values).astype(jnp.bfloat16)
    flat_att = attended.reshape(packs_here * rows, width_q)
    projected = jnp.dot(flat_att, full_weight, preferred_element_type=jnp.float32)
    projected = projected.astype(jnp.bfloat16).reshape(packs_here, rows, DM)
    factor = 1.0 / math.sqrt(packs_here * dp_count * rows * seq_count)
    piece_rows = width_q // (dp_count * seq_count)
    reordered = flat_att.reshape(packs_here * rows, dp_count, seq_count, piece_rows)
    reordered = reordered.transpose(0, 2, 1, 3).reshape(packs_here * rows, width_q)
    columns = lax.slice_in_dim(reordered, 0, piece_rows * lax.axis_size(("seq", "dp")), axis=1)
    summed = lax.psum_scatter(
        jnp.einsum("tq,td->qd", columns, flat_cot, preferred_element_type=jnp.float32),
        ("seq", "dp"),
        scatter_dimension=0,
        tiled=True,
    )
    grad_weight = lax.all_gather(summed, "seq", axis=0, tiled=True)
    grad_weight = grad_weight * factor
    return (projected, grad_queries, grad_keys, grad_values, grad_weight)


def solution(mesh):
    placed = (
        P("dp", "seq", None),
        P("dp", "seq", None),
        P("dp", "seq", None),
        P("dp", None),
        P("dp", None),
        P("dp", "seq", None),
    )
    return jax.shard_map(
        body,
        mesh=mesh,
        in_specs=placed,
        out_specs=(
            P("dp", "seq", None),
            P("dp", "seq", None),
            P("dp", "seq", None),
            P("dp", "seq", None),
            P("dp", None),
        ),
        check_vma=False,
    )
```

profile of v0, /device:TPU:1, one launch (start us, length us, event | category | flops | bytes accessed | tf_op | source)
XLA Modules:
  0.0 875.7 jit_solution(4079078539733141177)
XLA Ops:
  9.1 4.6 collective-permute-start
  13.7 1.9 collective-permute-start.1
  18.0 1.8 copy.261
  23.7 1.6 fusion.63
  29.8 1.3 copy-done.2
  31.5 73.4 %all-gather.3.cloned.1.call-done = bf16[2048,2048]{1,0:T(8,128)(2,1)} async-done(((bf16[256,2048]{1,0:T(8,128)(2,1)}), bf16[2048,2048]{1,0:T(8,128)(2,1)}) %all-gather.3.cloned.1.call-update) | async-done | bytes 8388624 | tf_op jit(solution)/shard_map/all_gather | solution.py:95
  104.9 5.7 fusion.1
  111.6 1.7 reshape.538
  113.3 1.7 reshape.550
  115.0 1.7 reshape.546
  116.8 1.7 reshape.542
  118.5 1.8 bitcast_convert_fusion.2
  120.3 2.0 copy.224
  122.3 1.8 bitcast_convert_fusion.1
  124.1 2.0 copy.233
  126.2 1.8 bitcast_convert_fusion
  128.0 2.0 copy.242
  130.0 1.8 bitcast_convert_fusion.3
  131.8 2.0 copy.215
  133.8 2.3 multiply_reduce_fusion
  141.5 8.1 fusion.34
  156.4 1.2 convolution_bitcast_fusion.2
  157.6 1.2 convolution_bitcast_fusion.1
  158.9 1.2 convolution_bitcast_fusion.3
  160.1 642.5 %reduce-scatter.2.cloned.1.call-done = f32[16,2048]{1,0:T(8,128)} async-done(((f32[2048,2048]{1,0:T(8,128)}), f32[16,2048]{1,0:T(8,128)}) %reduce-scatter.2.cloned.1.call-update) | async-done | bytes 131088 | tf_op jit(solution)/shard_map/reduce_scatter | solution.py:120
  802.6 1.2 pad_maximum_fusion.3
  805.0 1.6 fusion.15
  810.8 18.8 %collective-permute-start.2 = (bf16[1,256,512]{1,2,0:T(8,128)(2,1)}, bf16[1,256,512]{1,2,0:T(8,128)(2,1)}, u32[]{:S(2)}, u32[]{:S(2)}) collective-permute-start(bf16[1,256,512]{1,2,0:T(8,128)(2,1)} %slice.157), channel_id=1, source_target_pairs={{8,0},{16,8},{24,16},{32,24},{40,32},{48,40},{56,48},{64,56},{72,6... | collective-permute-start | bytes 786440 | tf_op jit(solution)/shard_map/ppermute | solution.py:17
  829.7 1.9 collective-permute-start.3
  832.6 6.7 fusion
  845.2 20.8 %all-gather.5.cloned.1.call-done = f32[256,2048]{1,0:T(8,128)} async-done(((f32[16,2048]{1,0:T(8,128)}), f32[256,2048]{1,0:T(8,128)}) %all-gather.5.cloned.1.call-update) | async-done | bytes 2097168 | tf_op jit(solution)/shard_map/all_gather | solution.py:126
  866.0 3.2 broadcast_multiply_fusion
  (180 shorter events, 37.7 us)
Async XLA Ops:
  7.2 97.7 %copy-start = (bf16[1,256,2048]{2,1,0:T(8,128)(2,1)S(1)}, bf16[1,256,2048]{2,1,0:T(8,128)(2,1)}, u32[]{:S(2)}) copy-start(bf16[1,256,2048]{2,1,0:T(8,128)(2,1)} %param.11) | copy-start | bytes 3145732
  7.2 10.0 %copy-start.40 = (bf16[1,256,2048]{2,1,0:T(8,128)(2,1)S(1)}, bf16[1,256,2048]{2,1,0:T(8,128)(2,1)}, u32[]{:S(2)}) copy-start(bf16[1,256,2048]{2,1,0:T(8,128)(2,1)} %param.6) | copy-start | bytes 3145732
  7.2 97.7 %all-gather.3.cloned.1.call-start = ((), (), s32[]{:S(2)}) async-start(), calls=%async_computation.1 | async-start | bytes 9437184 | tf_op jit(solution)/shard_map/all_gather | solution.py:95
  7.9 794.6 %reduce-scatter.2.cloned.1.call-start = ((), (), s32[]{:S(2)}) async-start(), calls=%async_computation.2 | async-start | bytes 16908288 | tf_op jit(solution)/shard_map/reduce_scatter | solution.py:120
  9.1 13.5 %collective-permute-start = (bf16[1,256,512]{1,2,0:T(8,128)(2,1)S(1)}, bf16[1,256,512]{1,2,0:T(8,128)(2,1)S(1)}, u32[]{:S(2)}, u32[]{:S(2)}) collective-permute-start(bf16[1,256,512]{1,2,0:T(8,128)(2,1)S(1)} %copy.152), channel_id=1, source_target_pairs={{0,8},{8,16},{16,24},{24,32},{32,40},{40,48},{48,56},{56,64},{64,7... | collective-permute-start | bytes 786440 | tf_op jit(solution)/shard_map/ppermute | solution.py:17
  13.7 8.9 %collective-permute-start.1 = (bf16[1,256,512]{2,1,0:T(8,128)(2,1)}, bf16[1,256,512]{2,1,0:T(8,128)(2,1)}, u32[]{:S(2)}, u32[]{:S(2)}) collective-permute-start(bf16[1,256,512]{2,1,0:T(8,128)(2,1)} %param.7), channel_id=1, source_target_pairs={{0,8},{8,16},{16,24},{24,32},{32,40},{40,48},{48,56},{56,64},{64,7... | collective-permute-start | bytes 786440 | tf_op jit(solution)/shard_map/ppermute | solution.py:17
  18.0 5.6 copy-start.52
  23.7 5.6 copy-start.18
  136.2 4.7 copy-start.41
  137.9 2.9 copy-start.46
  149.7 716.3 %all-gather.5.cloned.1.call-start = ((), (), s32[]{:S(2)}) async-start(), calls=%async_computation.3 | async-start | bytes 2228224 | tf_op jit(solution)/shard_map/all_gather | solution.py:126
  151.8 5.8 copy-start.34
  154.0 2.4 copy-start.16
  154.0 2.4 copy-start.11
  154.0 2.4 copy-start.36
  155.2 2.4 copy-start.7
  156.4 2.4 copy-start.4
  156.4 2.4 copy-start.33
  157.6 645.0 %copy-start.43 = (f32[1,512,128]{1,2,0:T(8,128)S(1)}, f32[1,512,128]{1,2,0:T(8,128)}, u32[]{:S(2)}) copy-start(f32[1,512,128]{1,2,0:T(8,128)} %convolution_bitcast_fusion) | copy-start | bytes 786436
  158.8 643.8 %copy-start.44 = (f32[1,512,128]{1,2,0:T(8,128)S(1)}, f32[1,512,128]{1,2,0:T(8,128)}, u32[]{:S(2)}) copy-start(f32[1,512,128]{1,2,0:T(8,128)} %convolution_bitcast_fusion.2) | copy-start | bytes 786436
  158.8 646.1 %copy-start.15 = (bf16[1,256,512]{1,2,0:T(8,128)(2,1)S(1)}, bf16[1,256,512]{1,2,0:T(8,128)(2,1)}, u32[]{:S(2)}) copy-start(bf16[1,256,512]{1,2,0:T(8,128)(2,1)} %copy-done.13) | copy-start | bytes 786436
  158.8 646.1 %copy-start.55 = (f32[4,256]{1,0:T(4,128)S(1)}, f32[4,256]{1,0:T(4,128)}, u32[]{:S(2)}) copy-start(f32[4,256]{1,0:T(4,128)} %get-tuple-element.45) | copy-start | bytes 12292
  809.5 22.1 %copy-start.17 = (bf16[4,256,512]{1,2,0:T(8,128)(2,1)S(1)}, bf16[4,256,512]{1,2,0:T(8,128)(2,1)}, u32[]{:S(2)}) copy-start(bf16[4,256,512]{1,2,0:T(8,128)(2,1)} %copy-done.16) | copy-start | bytes 3145732
  809.5 22.1 %copy-start.19 = (bf16[1,512,512]{2,1,0:T(8,128)(2,1)S(1)}, bf16[1,512,512]{2,1,0:T(8,128)(2,1)}, u32[]{:S(2)}) copy-start(bf16[1,512,512]{2,1,0:T(8,128)(2,1)} %copy-done.18) | copy-start | bytes 1572868
  810.8 21.8 %copy-start.42 = (bf16[128,4,256]{2,0,1:T(8,128)(2,1)S(1)}, bf16[128,4,256]{2,0,1:T(8,128)(2,1)}, u32[]{:S(2)}) copy-start(bf16[128,4,256]{2,0,1:T(8,128)(2,1)} %copy-done.41) | copy-start | bytes 786436
  810.8 21.8 %copy-start.47 = (bf16[128,4,256]{2,0,1:T(8,128)(2,1)S(1)}, bf16[128,4,256]{2,0,1:T(8,128)(2,1)}, u32[]{:S(2)}) copy-start(bf16[128,4,256]{2,0,1:T(8,128)(2,1)} %copy-done.46) | copy-start | bytes 786436
  810.8 21.8 %copy-start.49 = (bf16[128,4,256]{2,0,1:T(8,128)(2,1)S(1)}, bf16[128,4,256]{2,0,1:T(8,128)(2,1)}, u32[]{:S(2)}) copy-start(bf16[128,4,256]{2,0,1:T(8,128)(2,1)} %copy-done.48) | copy-start | bytes 786436
  810.8 21.8 %copy-start.51 = (bf16[128,4,256]{2,0,1:T(8,128)(2,1)S(1)}, bf16[128,4,256]{2,0,1:T(8,128)(2,1)}, u32[]{:S(2)}) copy-start(bf16[128,4,256]{2,0,1:T(8,128)(2,1)} %copy-done.50) | copy-start | bytes 786436
  810.8 30.6 %collective-permute-start.2 = (bf16[1,256,512]{1,2,0:T(8,128)(2,1)}, bf16[1,256,512]{1,2,0:T(8,128)(2,1)}, u32[]{:S(2)}, u32[]{:S(2)}) collective-permute-start(bf16[1,256,512]{1,2,0:T(8,128)(2,1)} %slice.157), channel_id=1, source_target_pairs={{8,0},{16,8},{24,16},{32,24},{40,32},{48,40},{56,48},{64,56},{72,6... | collective-permute-start | bytes 786440 | tf_op jit(solution)/shard_map/ppermute | solution.py:17
  829.7 13.6 %collective-permute-start.3 = (bf16[1,256,512]{1,2,0:T(8,128)(2,1)}, bf16[1,256,512]{1,2,0:T(8,128)(2,1)}, u32[]{:S(2)}, u32[]{:S(2)}) collective-permute-start(bf16[1,256,512]{1,2,0:T(8,128)(2,1)} %slice.156), channel_id=1, source_target_pairs={{8,0},{16,8},{24,16},{32,24},{40,32},{48,40},{56,48},{64,56},{72,6... | collective-permute-start | bytes 786440 | tf_op jit(solution)/shard_map/ppermute | solution.py:17
  840.1 3.2 copy-start.21
  844.3 24.8 %copy-start.1 = (bf16[1,256,2048]{2,1,0:T(8,128)(2,1)S(1)}, bf16[1,256,2048]{2,1,0:T(8,128)(2,1)}, u32[]{:S(2)}) copy-start(bf16[1,256,2048]{2,1,0:T(8,128)(2,1)} %param.11) | copy-start | bytes 3145732
  (31 other events, 51.9 us)
Sparse Core Ops, SparseCore 0:
  9.7 95.1 all-gather.2
  149.8 652.7 reduce-scatter.1
  805.0 60.9 all-gather.4
where the time goes:
time: 877 us; the launch traced here: 876 us
  waiting for transfers between devices  737 us (84%)
  matrix products  41.7 us (5%)
  local copies, waits for them, and re-layouts  36.5 us (4%)
  starting transfers between devices  27.6 us (3%)
  other arithmetic  18 us (2%)
  between operations  14.5 us (2%)
    reduce_scatter x1, waiting for transfers between devices, body(): lax.psum_scatter(jnp.einsum('tq,td->qd', columns, flat_cot, preferred_ele...  643 us
    all_gather x1, waiting for transfers between devices, body(): full_weight = lax.all_gather(out_weight, 'dp', axis=0, tiled=True)  73.4 us
    ppermute x4, starting transfers between devices, from_behind(): return lax.ppermute(value, axis, pairs)  27.3 us
    unnamed x124, local copies, waits for them, and re-layouts  23.5 us
    all_gather x1, waiting for transfers between devices, body(): grad_weight = lax.all_gather(summed, 'seq', axis=0, tiled=True)  20.8 us
  transfers between devices with their start and end apart: 7, of which 3 were waited for; matrix products, arithmetic and copies ran while one was open for 5% of the time, Pallas kernels for 0%

commit v1 on v0

v1 whole, which is shorter than its diff:
```python
import math

import jax
import jax.numpy as jnp
from jax import lax
from jax.experimental import pallas as pl
from jax.experimental.pallas import tpu as pltpu
from jax.sharding import PartitionSpec as P

HQ = 16
HK = 4
DH = 128
DM = 2048
TOK = 256
DOCS = 32
TOTAL = 32768
SCALE = 1.0 / math.sqrt(DH)
F32 = jnp.float32
BF16 = jnp.bfloat16
MESH = pl.DeviceIdType.MESH

HALO = 0
WX = HALO + 2
WZ = WX + 3
WC = WZ + 8
COT = WC + 7
ATT = COT + 1
Y1 = ATT + 4
X1 = Y1 + 12
Z1 = X1 + 3
Y2 = Z1 + 3
X2 = Y2 + 3
Z2 = X2 + 3
Y3 = Z2 + 3
X3 = Y3 + 3
Z3 = X3 + 3
BACK = Z3 + 3
AG = BACK + 2
AGC = AG + 7
COPIES = AGC + 8


def dg(a, b, ca, cb):
    return lax.dot_general(a, b, (((ca,), (cb,)), ((), ())), preferred_element_type=F32)


def kernel(
    len_ref, q_hbm, k_hbm, v_hbm, w_hbm, cot_hbm,
    pro_hbm, gq_hbm, gk_hbm, gv_hbm, gw_hbm,
    q_v, cot_v, kv, wf, cotm, att, attm, prob, bias,
    g_y, r_y1, s_y, r_y2, s_y2, r_y3,
    g_x, r_x1, s_x, r_x2, s_x2, r_x3,
    g_z, r_z1, s_z, r_z2, s_z2, r_z3,
    agb, gk_t, gv_t, back_s, back_r,
    pro_v, gq_v, gkv_v, gw_v,
    ssem, rsem, lsem, osem,
):
    s = lax.axis_index("seq")
    d = lax.axis_index("dp")
    zh = lax.div(s, 8)
    y = lax.rem(lax.div(s, 2), 4)
    c = lax.rem(s, 2)
    zl = lax.div(d, 4)
    x = lax.rem(d, 4)
    z = zh * 2 + zl

    def at(zh_, y_, c_, zl_, x_):
        return {"seq": zh_ * 8 + y_ * 2 + c_, "dp": zl_ * 4 + x_}

    def turn(v, n):
        return lax.rem(v + n, 4)

    def to_x(n):
        return at(zh, y, c, zl, turn(x, n))

    def to_y(n):
        return at(zh, turn(y, n), c, zl, x)

    def to_z(n):
        zz = turn(z, n)
        return at(lax.div(zz, 2), y, c, lax.rem(zz, 2), x)

    def to_o(n):
        return at(1 - zh, turn(y, n), c, zl, x)

    mate = at(zh, y, 1 - c, zl, x)
    near = at(zh, y, c, 1 - zl, x)
    far = at(1 - zh, y, c, 1 - zl, x)
    after = {"seq": lax.rem(s + 1, 16), "dp": d}
    before = {"seq": lax.rem(s + 15, 16), "dp": d}

    def rc(n, src, dst, to):
        return pltpu.make_async_remote_copy(
            src_ref=src, dst_ref=dst, send_sem=ssem.at[n], recv_sem=rsem.at[n],
            device_id=to, device_id_type=MESH,
        )

    sent = []

    def send(n, src, dst, to):
        copy = rc(n, src, dst, to)
        copy.start()
        sent.append(copy)

    loads = [
        pltpu.make_async_copy(k_hbm, kv.at[0, pl.ds(TOK, TOK)], lsem.at[0]),
        pltpu.make_async_copy(v_hbm, kv.at[1, pl.ds(TOK, TOK)], lsem.at[1]),
        pltpu.make_async_copy(q_hbm, q_v, lsem.at[2]),
        pltpu.make_async_copy(cot_hbm, cot_v, lsem.at[3]),
        pltpu.make_async_copy(w_hbm, wf.at[d], lsem.at[4]),
    ]
    for load in loads:
        load.start()

    barrier = pltpu.get_barrier_semaphore()
    peers = [mate, after, before]
    peers += [f(n) for f in (to_x, to_y, to_z) for n in (1, 2, 3)]
    peers += [to_o(n) for n in (1, 2, 3)]
    for peer in peers:
        pl.semaphore_signal(barrier, inc=1, device_id=peer, device_id_type=MESH)
    pl.semaphore_wait(barrier, len(peers))

    prev = pl.ds(0, TOK)
    send(HALO, k_hbm, kv.at[0, prev], after)
    send(HALO + 1, v_hbm, kv.at[1, prev], after)
    way = (1, 3, 2)
    for i, n in enumerate(way):
        send(WX + i, w_hbm.at[c], wf.at[d, c], to_x(n))
    low, high = pl.ds(0, 64), pl.ds(64, 64)
    send(WZ, w_hbm.at[c, low], wf.at[d, c, low], near)
    send(WZ + 1, w_hbm.at[c, high], wf.at[d, c, high], far)
    send(COT, cot_hbm.at[:, pl.ds(pl.multiple_of((1 - c) * 1024, 1024), 1024)], cotm, mate)

    def shard_x(i, plane):
        return plane * 4 + (x if i == 0 else turn(x, 4 - way[i - 1]))

    def forward_x(i):
        e = shard_x(i, zl)
        rc(WX + i - 1, w_hbm.at[c], wf.at[e, c], mate).wait_recv()
        send(WZ + 2 * i, wf.at[e, c, low], wf.at[e, c, low], near)
        send(WZ + 2 * i + 1, wf.at[e, c, high], wf.at[e, c, high], far)
        send(WC + i - 1, wf.at[e, c], wf.at[e, c], mate)

    def forward_z(i):
        e = shard_x(i, 1 - zl)
        rc(WZ + 2 * i, w_hbm.at[c, low], wf.at[e, c, low], mate).wait_recv()
        rc(WZ + 2 * i + 1, w_hbm.at[c, high], wf.at[e, c, high], mate).wait_recv()
        send(WC + 3 + i, wf.at[e, c], wf.at[e, c], mate)

    def from_mate(j, e):
        rc(WC + j, wf.at[e, 1 - c], wf.at[e, 1 - c], mate).wait_recv()

    first = s * TOK
    q_pos = first + lax.broadcasted_iota(jnp.int32, (TOK, 1), 0)
    begin = jnp.zeros((TOK, 1), jnp.int32)
    opening = len_ref[0, 0] * 0
    for n in range(DOCS):
        begin = jnp.where(q_pos >= opening, opening, begin)
        opening = opening + len_ref[0, n]
    k_pos = first - TOK + lax.broadcasted_iota(jnp.int32, (TOK, 2 * TOK), 1)
    bias[...] = jnp.where((k_pos >= begin) & (k_pos <= q_pos), 0.0, -1e30)
    gk_t[...] = jnp.zeros_like(gk_t)
    gv_t[...] = jnp.zeros_like(gv_t)

    for load in loads:
        load.wait()
    rc(HALO, k_hbm, kv.at[0, prev], after).wait_recv()
    rc(HALO + 1, v_hbm, kv.at[1, prev], after).wait_recv()

    def head(h):
        return pl.ds(pl.multiple_of(h * DH, DH), DH)

    def fwd(k):
        keys, values = kv[0, :, head(k)], kv[1, :, head(k)]

        def one(g, _):
            h = k * 4 + g
            scores = dg(q_v[:, head(h)], keys, 1, 1) * SCALE + bias[...]
            e = jnp.exp(scores - jnp.max(scores, axis=-1, keepdims=True))
            p = (e * (1.0 / jnp.sum(e, axis=-1, keepdims=True))).astype(BF16)
            prob[h] = p
            att[:, head(h)] = dg(p, values, 1, 0).astype(BF16)
            return 0

        lax.fori_loop(0, 4, one, 0)
        cols = pl.ds(k * 512, 512)
        send(ATT + k, att.at[:, cols], attm.at[:, cols], mate)

    def grad_w(k):
        cols = pl.ds(k * 512, 512)
        rc(ATT + k, att.at[:, cols], attm.at[:, cols], mate).wait_recv()
        if k == 0:
            rc(COT, cotm, cotm, mate).wait_recv()
        for e in (2 * k, 2 * k + 1):
            own = att[:, e * 256 : (e + 1) * 256]
            other = attm[:, e * 256 : (e + 1) * 256]
            for n in range(4):
                mine = cot_v[:, pl.ds(pl.multiple_of(c * 1024 + n * 256, 256), 256)]
                part = dg(own, mine, 0, 0) + dg(other, cotm[:, n * 256 : (n + 1) * 256], 0, 0)
                part = part.astype(BF16)
                for sub in range(8):
                    rows = part[sub * 32 : (sub + 1) * 32]
                    if n < 2:
                        g_y[sub % 4, e, sub // 4, :, n * 256 : (n + 1) * 256] = rows
                    elif n == 2:
                        g_x[e % 4, e // 4, sub] = rows
                    else:
                        g_z[sub // 4 * 2 + e // 4, e % 4, sub % 4] = rows
        both = pl.ds(2 * k, 2)
        for n in (1, 3, 2):
            send(Y1 + 3 * k + n - 1, g_y.at[turn(y, n), both], r_y1.at[n - 1, both], to_y(n))

    for k in range(HK):
        fwd(k)
        if k > 0:
            grad_w(k - 1)
        if k == 2:
            forward_x(1)
        if k == 3:
            forward_x(2)
    grad_w(HK - 1)
    forward_x(3)
    for n in (1, 3, 2):
        send(X1 + n - 1, g_x.at[turn(x, n)], r_x1.at[n - 1], to_x(n))
        send(Z1 + n - 1, g_z.at[turn(z, n)], r_z1.at[n - 1], to_z(n))

    def bwd(e):
        k = lax.div(e, 2)
        weight = wf[e].reshape(256, DM)
        grad = dg(cot_v[...], weight, 1, 1).astype(BF16)
        keys, values = kv[0, :, head(k)], kv[1, :, head(k)]
        for g in range(2):
            h = 2 * e + g
            grad_h = grad[:, g * DH : (g + 1) * DH]
            delta = jnp.sum(
                grad_h.astype(F32) * att[:, head(h)].astype(F32), axis=-1, keepdims=True
            )
            p = prob[h]
            grad_s = (p.astype(F32) * (dg(grad_h, values, 1, 1) - delta)).astype(BF16)
            gq_v[:, head(h)] = (dg(grad_s, keys, 1, 0) * SCALE).astype(BF16)
            gk_t[head(k), :] += dg(q_v[:, head(h)], grad_s, 0, 0)
            gv_t[head(k), :] += dg(grad_h, p, 0, 0)

    bwd(d)
    for i in range(1, 4):
        e = shard_x(i, zl)
        if i == 1:
            forward_z(0)
        from_mate(i - 1, e)
        bwd(e)
    for i in range(4):
        e = shard_x(i, 1 - zl)
        if i < 3:
            forward_z(i + 1)
        from_mate(3 + i, e)
        bwd(e)

    back_s[0] = (gk_t[:, 0:TOK].T * SCALE).astype(BF16)
    back_s[1] = gv_t[:, 0:TOK].T.astype(BF16)
    send(BACK, back_s.at[0], back_r.at[0], before)
    send(BACK + 1, back_s.at[1], back_r.at[1], before)

    def arrived(base, dst, source):
        for n in range(3):
            rc(base + n, source, dst.at[n], mate).wait_recv()

    def total(own, got, *where):
        out = own.astype(F32)
        for n in range(3):
            out = out + got[(n, *where)].astype(F32)
        return out

    arrived(X1, r_x1, g_x.at[0])
    for zl_ in range(2):
        for sub in range(8):
            value = total(g_x[x, zl_, sub], r_x1, zl_, sub)
            s_x[sub // 4 * 2 + zl_, sub % 4] = value.astype(BF16)
    for n in (1, 3, 2):
        send(Z2 + n - 1, s_x.at[turn(z, n)], r_x2.at[n - 1], to_z(n))

    arrived(Z1, r_z1, g_z.at[0])
    for x_ in range(4):
        for y_ in range(4):
            s_z[y_, x_] = total(g_z[z, x_, y_], r_z1, x_, y_).astype(BF16)
    for n in (1, 3, 2):
        send(Y2 + n - 1, s_z.at[turn(y, n)], r_z2.at[n - 1], to_y(n))

    for k in range(HK):
        both = pl.ds(2 * k, 2)
        for n in range(3):
            rc(Y1 + 3 * k + n, g_y.at[0, both], r_y1.at[n, both], mate).wait_recv()
    for e in range(8):
        for zh_ in range(2):
            s_y[e % 4, e // 4, zh_] = total(g_y[y, e, zh_], r_y1, e, zh_).astype(BF16)
    for n in (1, 3, 2):
        send(X2 + n - 1, s_y.at[turn(x, n)], r_y2.at[n - 1], to_x(n))

    def project(n, _):
        cols = pl.ds(pl.multiple_of(n * 256, 256), 256)
        weight = wf[:, :, :, cols].reshape(2048, 256)
        pro_v[:, cols] = dg(att[...], weight, 1, 0).astype(BF16)
        return 0

    lax.fori_loop(0, 8, project, 0)
    outs = [
        pltpu.make_async_copy(pro_v, pro_hbm, osem.at[0]),
        pltpu.make_async_copy(gq_v, gq_hbm, osem.at[1]),
    ]
    for out in outs:
        out.start()

    arrived(Z2, r_x2, s_x.at[0])
    for y_ in range(4):
        s_x2[y_] = total(s_x[z, y_], r_x2, y_).astype(BF16)
    for n in (1, 3, 2):
        send(Y3 + n - 1, s_x2.at[turn(y, n)], r_x3.at[n - 1], to_y(n))
    arrived(Y2, r_z2, s_z.at[0])
    for x_ in range(4):
        s_z2[x_] = total(s_z[y, x_], r_z2, x_).astype(BF16)
    for n in (1, 3, 2):
        send(X3 + n - 1, s_z2.at[turn(x, n)], r_z3.at[n - 1], to_x(n))
    arrived(X2, r_y2, s_y.at[0])
    for zl_ in range(2):
        for zh_ in range(2):
            s_y2[zh_ * 2 + zl_] = total(s_y[x, zl_, zh_], r_y2, zl_, zh_).astype(BF16)
    for n in (1, 3, 2):
        send(Z3 + n - 1, s_y2.at[turn(z, n)], r_y3.at[n - 1], to_z(n))

    factor = 1.0 / math.sqrt(TOTAL)
    mine = zh * 4 + y
    arrived(Y3, r_x3, s_x2.at[0])
    agb[c, mine, :, 512:768] = (total(s_x2[y], r_x3) * factor).astype(BF16)
    arrived(X3, r_z3, s_z2.at[0])
    agb[c, mine, :, 768:1024] = (total(s_z2[x], r_z3) * factor).astype(BF16)
    arrived(Z3, r_y3, s_y2.at[0])
    agb[c, mine, :, 0:512] = (total(s_y2[z], r_y3) * factor).astype(BF16)

    for n in range(7):
        to = to_y(n + 1) if n < 3 else to_o(n - 3)
        send(AG + n, agb.at[c, mine], agb.at[c, mine], to)
    send(AGC + 7, agb.at[c, mine], agb.at[c, mine], mate)

    rc(BACK, back_s.at[0], back_r.at[0], before).wait_recv()
    rc(BACK + 1, back_s.at[1], back_r.at[1], before).wait_recv()
    gkv_v[0] = (gk_t[:, TOK : 2 * TOK].T * SCALE + back_r[0].astype(F32)).astype(BF16)
    gkv_v[1] = (gv_t[:, TOK : 2 * TOK].T + back_r[1].astype(F32)).astype(BF16)
    for n, out in enumerate((gk_hbm, gv_hbm)):
        outs.append(pltpu.make_async_copy(gkv_v.at[n], out, osem.at[2 + n]))
        outs[-1].start()

    def origin(n):
        if n == 7:
            return mine
        return zh * 4 + turn(y, 3 - n) if n < 3 else (1 - zh) * 4 + turn(y, 7 - n)

    for n in range(7):
        piece = agb.at[c, origin(n)]
        rc(AG + n, piece, piece, mate).wait_recv()
        send(AGC + n, piece, piece, mate)
    for n in range(8):
        piece = agb.at[1 - c, origin(n)]
        rc(AGC + n, piece, piece, mate).wait_recv()
    for sub in range(8):
        for half in range(2):
            gw_v[sub * 32 : (sub + 1) * 32, half * 1024 : (half + 1) * 1024] = agb[
                half, sub
            ].astype(F32)
    outs.append(pltpu.make_async_copy(gw_v, gw_hbm, osem.at[4]))
    outs[-1].start()
    for copy in sent:
        copy.wait_send()
    for out in outs:
        out.wait()


def body(queries, key_heads, value_heads, doc_lengths, out_weight, cotangent):
    anywhere = pl.BlockSpec(memory_space=pl.ANY)
    shapes = [
        ((TOK, 2048), BF16),
        ((TOK, 2048), BF16),
        ((2, 512, 512), BF16),
        ((8, 2, 128, 2048), BF16),
        ((TOK, 1024), BF16),
        ((TOK, 2048), BF16),
        ((TOK, 2048), BF16),
        ((HQ, TOK, 512), BF16),
        ((TOK, 512), F32),
        ((4, 8, 2, 32, 512), BF16),
        ((3, 8, 2, 32, 512), BF16),
        ((4, 2, 2, 32, 512), BF16),
        ((3, 2, 2, 32, 512), BF16),
        ((4, 32, 512), BF16),
        ((3, 32, 512), BF16),
        ((4, 2, 8, 32, 256), BF16),
        ((3, 2, 8, 32, 256), BF16),
        ((4, 4, 32, 256), BF16),
        ((3, 4, 32, 256), BF16),
        ((4, 32, 256), BF16),
        ((3, 32, 256), BF16),
        ((4, 4, 4, 32, 256), BF16),
        ((3, 4, 4, 32, 256), BF16),
        ((4, 4, 32, 256), BF16),
        ((3, 4, 32, 256), BF16),
        ((4, 32, 256), BF16),
        ((3, 32, 256), BF16),
        ((2, 8, 32, 1024), BF16),
        ((512, 512), F32),
        ((512, 512), F32),
        ((2, TOK, 512), BF16),
        ((2, TOK, 512), BF16),
        ((TOK, 2048), BF16),
        ((TOK, 2048), BF16),
        ((2, TOK, 512), BF16),
        ((TOK, 2048), F32),
    ]
    scratch = [pltpu.VMEM(shape, dtype) for shape, dtype in shapes]
    scratch += [pltpu.SemaphoreType.DMA((n,)) for n in (COPIES, COPIES, 5, 5)]
    outs = pl.pallas_call(
        kernel,
        out_shape=[
            jax.ShapeDtypeStruct((TOK, 2048), BF16),
            jax.ShapeDtypeStruct((TOK, 2048), BF16),
            jax.ShapeDtypeStruct((TOK, 512), BF16),
            jax.ShapeDtypeStruct((TOK, 512), BF16),
            jax.ShapeDtypeStruct((TOK, 2048), F32),
        ],
        in_specs=[pl.BlockSpec(memory_space=pltpu.SMEM)] + [anywhere] * 5,
        out_specs=[anywhere] * 5,
        scratch_shapes=scratch,
        compiler_params=pltpu.CompilerParams(
            collective_id=0, has_side_effects=True, vmem_limit_bytes=56 << 20
        ),
        cost_estimate=pl.CostEstimate(
            flops=10_000_000_000, bytes_accessed=12_000_000, transcendentals=2_000_000
        ),
    )(
        doc_lengths,
        queries[0],
        key_heads[0],
        value_heads[0],
        out_weight.reshape(2, 128, DM),
        cotangent[0],
    )
    return (*(out[None] for out in outs[:4]), outs[4])


def solution(mesh):
    tokens = P("dp", "seq", None)
    rows = P("dp", None)
    return jax.shard_map(
        body,
        mesh=mesh,
        in_specs=(tokens, tokens, tokens, rows, rows, tokens),
        out_specs=(tokens, tokens, tokens, tokens, rows),
        check_vma=False,
    )
```

time: 877 us -> 89.6 us (0.10)
  waiting for transfers between devices: 737 us -> 0 us
  Pallas kernels: 0 us -> 82.6 us
  matrix products: 41.7 us -> 0 us
  local copies, waits for them, and re-layouts: 36.5 us -> 6.13 us
  starting transfers between devices: 27.6 us -> 0 us
  other arithmetic: 18 us -> 0 us
  between operations: 14.5 us -> 0.67 us
    reduce_scatter x1 -> x0, waiting for transfers between devices: 643 us -> none  [body(): lax.psum_scatter(jnp.einsum('tq,td->qd', columns, flat_cot, preferred_ele...]
    all_gather x2 -> x0, waiting for transfers between devices: 94.2 us -> none  [the longest x1 73.4 us: body(): full_weight = lax.all_gather(out_weight, 'dp', axis=0, tiled=True)]
    pallas_call x0 -> x1, Pallas kernels: none -> 82.6 us  [body(): pl.pallas_call(kernel, out_shape=[jax.ShapeDtypeStruct((TOK, 2048), BF16)...]
    dot_general x27 -> x0, matrix products: 41.7 us -> none  [the longest x1 8.1 us: body(): jnp.einsum('tq,td->qd', columns, flat_cot, preferred_element_type=jnp.flo...]
    ppermute x4 -> x0, starting transfers between devices: 27.3 us -> none  [from_behind(): return lax.ppermute(value, axis, pairs)]
    unnamed x124 -> x13, local copies, waits for them, and re-layouts: 23.5 us -> 6.13 us
    another operation x8 -> x0, local copies, waits for them, and re-layouts: 9.01 us -> none
  transfers between devices with their start and end apart: 7 -> 0, of which waited for: 3 -> 0; matrix products, arithmetic and copies ran while one was open for 5% -> 0% of each run, Pallas kernels for 0% -> 0%
where the time goes in v1:
time: 89.6 us; the launch traced here: 89.4 us
  Pallas kernels  82.6 us (92%)
  local copies, waits for them, and re-layouts  6.13 us (7%)
    pallas_call x1, Pallas kernels, body(): pl.pallas_call(kernel, out_shape=[jax.ShapeDtypeStruct((TOK, 2048), BF16)...  82.6 us
    unnamed x13, local copies, waits for them, and re-layouts  6.13 us

profile of v1, /device:TPU:1, one launch (start us, length us, event | category | flops | bytes accessed | tf_op | source)
XLA Modules:
  0.0 89.4 jit_solution(6101328698853435521)
XLA Ops:
  0.6 82.6 %shard_map.101 = (bf16[256,2048]{1,0:T(8,128)(2,1)}, bf16[256,2048]{1,0:T(8,128)(2,1)}, bf16[256,512]{1,0:T(8,128)(2,1)}, bf16[256,512]{1,0:T(8,128)(2,1)}, f32[256,2048]{1,0:T(8,128)}) custom-call(s32[1,32]{1,0:T(1,128)} %len_ref.1, bf16[256,2048]{1,0:T(8,128)(2,1)} %bitcast.13, bf16[256,512]{1,0:T(8,128)(2,1)} %bitcast.16, bf16[256,512]{1,0:T(8,128)(2,1)} %bitcast.17, ...), custom_call_target="tpu_custom_call" | custom-call | flops 10000000000 | bytes 12000000 | tf_op jit(solution)/shard_map/pallas_call | solution.py:418
  83.3 0.0 copy-start.1
  83.3 0.0 copy-start.3
  83.3 0.0 copy-start.2
  83.3 2.4 %copy.16 = bf16[1,256,2048]{2,1,0:T(8,128)(2,1)} copy(bf16[1,256,2048]{2,1,0:T(8,128)(2,1)} %bitcast.10) | data formatting | bytes 2097152
  85.7 0.0 copy-done.1
  85.7 0.0 copy-start
  85.7 1.0 %copy.17 = bf16[1,256,2048]{2,1,0:T(8,128)(2,1)} copy(bf16[1,256,2048]{2,1,0:T(8,128)(2,1)S(1)} %bitcast.9) | data formatting | bytes 2097152
  86.7 0.0 copy-done.3
  86.7 0.7 copy.18
  87.4 0.0 copy-done.2
  87.4 0.7 copy.19
  88.1 0.0 copy-done
  88.1 1.3 %copy.20 = f32[256,2048]{1,0:T(8,128)} copy(f32[256,2048]{1,0:T(8,128)S(1)} %copy-done) | data formatting | bytes 4194304
Async XLA Ops:
  83.3 2.5 %copy-start.1 = (bf16[256,2048]{1,0:T(8,128)(2,1)S(1)}, bf16[256,2048]{1,0:T(8,128)(2,1)}, u32[]{:S(2)}) copy-start(bf16[256,2048]{1,0:T(8,128)(2,1)} %get-tuple-element.11) | copy-start | bytes 3145732
  83.3 3.4 %copy-start.3 = (bf16[256,512]{1,0:T(8,128)(2,1)S(1)}, bf16[256,512]{1,0:T(8,128)(2,1)}, u32[]{:S(2)}) copy-start(bf16[256,512]{1,0:T(8,128)(2,1)} %get-tuple-element.12) | copy-start | bytes 786436
  83.3 4.1 %copy-start.2 = (bf16[256,512]{1,0:T(8,128)(2,1)S(1)}, bf16[256,512]{1,0:T(8,128)(2,1)}, u32[]{:S(2)}) copy-start(bf16[256,512]{1,0:T(8,128)(2,1)} %get-tuple-element.13) | copy-start | bytes 786436
  85.7 2.4 %copy-start = (f32[256,2048]{1,0:T(8,128)S(1)}, f32[256,2048]{1,0:T(8,128)}, u32[]{:S(2)}) copy-start(f32[256,2048]{1,0:T(8,128)} %get-tuple-element.24) | copy-start | bytes 6291460

commit v2 on v1

v2 whole, which is shorter than its diff:
```python
import math

import jax
import jax.numpy as jnp
from jax import lax
from jax.experimental import pallas as pl
from jax.experimental.pallas import tpu as pltpu
from jax.sharding import PartitionSpec as P

HQ = 16
HK = 4
DH = 128
DM = 2048
TOK = 256
DOCS = 32
TOTAL = 32768
SCALE = 1.0 / math.sqrt(DH)
F32 = jnp.float32
BF16 = jnp.bfloat16
MESH = pl.DeviceIdType.MESH

HALO = 0
WX = HALO + 8
WZ = WX + 6
WC = WZ + 8
COT = WC + 7
ATT = COT + 1
Y1 = ATT + 4
X1 = Y1 + 12
Z1 = X1 + 3
Y2 = Z1 + 3
X2 = Y2 + 3
Z2 = X2 + 3
Y3 = Z2 + 3
X3 = Y3 + 3
Z3 = X3 + 3
BACK = Z3 + 3
AG = BACK + 2
AGC = AG + 14
COPIES = AGC + 2


def dg(a, b, ca, cb):
    return lax.dot_general(a, b, (((ca,), (cb,)), ((), ())), preferred_element_type=F32)


def kernel(
    len_ref, q_hbm, k_hbm, v_hbm, w_hbm, cot_hbm,
    pro_hbm, gq_hbm, gk_hbm, gv_hbm, gw_hbm,
    q_v, cot_v, kv, wf, cotm, att, attm, prob, bias,
    g_y, r_y1, s_y, r_y2, s_y2, r_y3,
    g_x, r_x1, s_x, r_x2, s_x2, r_x3,
    g_z, r_z1, s_z, r_z2, s_z2, r_z3,
    agb, gk_t, gv_t, back_s, back_r,
    pro_v, gq_v, gkv_v,
    ssem, rsem, lsem, osem,
):
    s = lax.axis_index("seq")
    d = lax.axis_index("dp")
    zh = lax.div(s, 8)
    y = lax.rem(lax.div(s, 2), 4)
    c = lax.rem(s, 2)
    zl = lax.div(d, 4)
    x = lax.rem(d, 4)
    z = zh * 2 + zl

    def at(zh_, y_, c_, zl_, x_):
        return {"seq": zh_ * 8 + y_ * 2 + c_, "dp": zl_ * 4 + x_}

    def turn(v, n):
        return lax.rem(v + n, 4)

    def to_x(n):
        return at(zh, y, c, zl, turn(x, n))

    def to_y(n):
        return at(zh, turn(y, n), c, zl, x)

    def to_z(n):
        zz = turn(z, n)
        return at(lax.div(zz, 2), y, c, lax.rem(zz, 2), x)

    def to_o(n):
        return at(1 - zh, turn(y, n), c, zl, x)

    mate = at(zh, y, 1 - c, zl, x)
    near = at(zh, y, c, 1 - zl, x)
    far = at(1 - zh, y, c, 1 - zl, x)
    after = {"seq": lax.rem(s + 1, 16), "dp": d}
    before = {"seq": lax.rem(s + 15, 16), "dp": d}

    def rc(n, src, dst, to):
        return pltpu.make_async_remote_copy(
            src_ref=src, dst_ref=dst, send_sem=ssem.at[n], recv_sem=rsem.at[n],
            device_id=to, device_id_type=MESH,
        )

    sent = []

    def send(n, src, dst, to):
        copy = rc(n, src, dst, to)
        copy.start()
        sent.append(copy)

    loads = [
        pltpu.make_async_copy(k_hbm, kv.at[0, pl.ds(TOK, TOK)], lsem.at[0]),
        pltpu.make_async_copy(v_hbm, kv.at[1, pl.ds(TOK, TOK)], lsem.at[1]),
        pltpu.make_async_copy(q_hbm, q_v, lsem.at[2]),
        pltpu.make_async_copy(cot_hbm, cot_v, lsem.at[3]),
        pltpu.make_async_copy(w_hbm, wf.at[d], lsem.at[4]),
    ]
    for load in loads:
        load.start()

    barrier = pltpu.get_barrier_semaphore()
    peers = [mate, after, before]
    peers += [f(n) for f in (to_x, to_y, to_z) for n in (1, 2, 3)]
    peers += [to_o(n) for n in (1, 2, 3)]
    for peer in peers:
        pl.semaphore_signal(barrier, inc=1, device_id=peer, device_id_type=MESH)

    first = s * TOK
    q_pos = first + lax.broadcasted_iota(jnp.int32, (TOK, 1), 0)
    begin = jnp.zeros((TOK, 1), jnp.int32)
    opening = len_ref[0, 0] * 0
    for n in range(DOCS):
        begin = jnp.where(q_pos >= opening, opening, begin)
        opening = opening + len_ref[0, n]
    k_pos = first - TOK + lax.broadcasted_iota(jnp.int32, (TOK, 2 * TOK), 1)
    bias[...] = jnp.where((k_pos >= begin) & (k_pos <= q_pos), 0.0, -1e30)
    gk_t[...] = jnp.zeros_like(gk_t)
    gv_t[...] = jnp.zeros_like(gv_t)

    pl.semaphore_wait(barrier, len(peers))

    prev = pl.ds(0, TOK)
    low, high = pl.ds(0, 64), pl.ds(64, 64)

    def halo(n):
        cols = pl.ds(n // 2 * DH, DH)
        source = (k_hbm, v_hbm)[n % 2]
        return HALO + n, source.at[:, cols], kv.at[n % 2, prev, cols], after

    for n in range(8):
        send(*halo(n))
    send(WX, w_hbm.at[c, low], wf.at[d, c, low], to_x(1))
    send(WX + 2, w_hbm.at[c, high], wf.at[d, c, high], to_x(3))
    send(WX + 1, w_hbm.at[c, high], wf.at[d, c, high], to_x(1))
    send(WX + 3, w_hbm.at[c, low], wf.at[d, c, low], to_x(3))
    send(WZ, w_hbm.at[c, low], wf.at[d, c, low], near)
    send(WZ + 1, w_hbm.at[c, high], wf.at[d, c, high], far)
    send(COT, cot_hbm.at[:, pl.ds(pl.multiple_of((1 - c) * 1024, 1024), 1024)], cotm, mate)

    def shard_x(i, plane):
        return plane * 4 + turn(x, (0, 3, 1, 2)[i])

    def part_x(n, i, part, relay=None):
        piece = wf.at[shard_x(i, zl), c, part]
        rc(WX + n, piece, piece, mate).wait_recv()
        if relay is not None:
            send(WX + relay[0], piece, piece, to_x(relay[1]))
        if part is low:
            send(WZ + 2 * i, piece, piece, near)
        else:
            send(WZ + 2 * i + 1, piece, piece, far)

    def to_mate(j, e):
        send(WC + j, wf.at[e, c], wf.at[e, c], mate)

    def forward_x(step):
        if step == 0:
            part_x(0, 1, low, (4, 1))
            part_x(2, 2, high, (5, 3))
        if step == 1:
            part_x(1, 1, high)
            part_x(3, 2, low)
            to_mate(0, shard_x(1, zl))
            to_mate(1, shard_x(2, zl))
        if step == 2:
            part_x(4, 3, low)
            part_x(5, 3, high)
            to_mate(2, shard_x(3, zl))

    def forward_z(i):
        e = shard_x(i, 1 - zl)
        rc(WZ + 2 * i, wf.at[e, c, low], wf.at[e, c, low], mate).wait_recv()
        rc(WZ + 2 * i + 1, wf.at[e, c, high], wf.at[e, c, high], mate).wait_recv()
        to_mate(3 + i, e)

    def from_mate(j, e):
        rc(WC + j, wf.at[e, 1 - c], wf.at[e, 1 - c], mate).wait_recv()

    for load in loads[:3]:
        load.wait()

    def head(h):
        return pl.ds(pl.multiple_of(h * DH, DH), DH)

    def fwd(k):
        for n in (2 * k, 2 * k + 1):
            rc(*halo(n)).wait_recv()
        keys, values = kv[0, :, head(k)], kv[1, :, head(k)]

        def one(g, _):
            h = k * 4 + g
            scores = dg(q_v[:, head(h)], keys, 1, 1) * SCALE + bias[...]
            e = jnp.exp(scores - jnp.max(scores, axis=-1, keepdims=True))
            p = (e * (1.0 / jnp.sum(e, axis=-1, keepdims=True))).astype(BF16)
            prob[h] = p
            att[:, head(h)] = dg(p, values, 1, 0).astype(BF16)
            return 0

        lax.fori_loop(0, 4, one, 0)
        cols = pl.ds(k * 512, 512)
        send(ATT + k, att.at[:, cols], attm.at[:, cols], mate)

    def grad_w(k):
        cols = pl.ds(k * 512, 512)
        rc(ATT + k, att.at[:, cols], attm.at[:, cols], mate).wait_recv()
        if k == 0:
            loads[3].wait()
            rc(COT, cotm, cotm, mate).wait_recv()
        for e in (2 * k, 2 * k + 1):
            own = att[:, e * 256 : (e + 1) * 256]
            other = attm[:, e * 256 : (e + 1) * 256]
            for n in range(4):
                mine = cot_v[:, pl.ds(pl.multiple_of(c * 1024 + n * 256, 256), 256)]
                part = dg(own, mine, 0, 0) + dg(other, cotm[:, n * 256 : (n + 1) * 256], 0, 0)
                part = part.astype(BF16)
                for sub in range(8):
                    rows = part[sub * 32 : (sub + 1) * 32]
                    if n < 2:
                        g_y[sub % 4, e, sub // 4, :, n * 256 : (n + 1) * 256] = rows
                    elif n == 2:
                        g_x[e % 4, e // 4, sub, :, 0:256] = rows
                    else:
                        g_x[e % 4, e // 4, sub, :, 256:384] = rows[:, 0:128]
                        g_z[sub // 4 * 2 + e // 4, e % 4, sub % 4] = rows[:, 128:256]
        both = pl.ds(2 * k, 2)
        for n in (1, 3, 2):
            send(Y1 + 3 * k + n - 1, g_y.at[turn(y, n), both], r_y1.at[n - 1, both], to_y(n))

    fwd(0)
    fwd(1)
    grad_w(0)
    forward_x(0)
    fwd(2)
    grad_w(1)
    forward_x(1)
    fwd(3)
    grad_w(2)
    forward_x(2)
    grad_w(3)
    for n in (1, 3, 2):
        send(X1 + n - 1, g_x.at[turn(x, n)], r_x1.at[n - 1], to_x(n))
        send(Z1 + n - 1, g_z.at[turn(z, n)], r_z1.at[n - 1], to_z(n))
    loads[4].wait()

    def bwd(e):
        k = lax.div(e, 2)
        weight = wf[e].reshape(256, DM)
        grad = dg(cot_v[...], weight, 1, 1).astype(BF16)
        keys, values = kv[0, :, head(k)], kv[1, :, head(k)]
        for g in range(2):
            h = 2 * e + g
            grad_h = grad[:, g * DH : (g + 1) * DH]
            delta = jnp.sum(
                grad_h.astype(F32) * att[:, head(h)].astype(F32), axis=-1, keepdims=True
            )
            p = prob[h]
            grad_s = (p.astype(F32) * (dg(grad_h, values, 1, 1) - delta)).astype(BF16)
            gq_v[:, head(h)] = (dg(grad_s, keys, 1, 0) * SCALE).astype(BF16)
            gk_t[head(k), :] += dg(q_v[:, head(h)], grad_s, 0, 0)
            gv_t[head(k), :] += dg(grad_h, p, 0, 0)

    bwd(d)
    for i in range(1, 4):
        e = shard_x(i, zl)
        if i == 1:
            forward_z(0)
        from_mate(i - 1, e)
        bwd(e)
    for i in range(4):
        e = shard_x(i, 1 - zl)
        if i < 3:
            forward_z(i + 1)
        from_mate(3 + i, e)
        bwd(e)

    back_s[0] = (gk_t[:, 0:TOK].T * SCALE).astype(BF16)
    back_s[1] = gv_t[:, 0:TOK].T.astype(BF16)
    send(BACK, back_s.at[0], back_r.at[0], before)
    send(BACK + 1, back_s.at[1], back_r.at[1], before)

    def arrived(base, dst, source):
        for n in range(3):
            rc(base + n, source, dst.at[n], mate).wait_recv()

    def total(own, got, *where):
        out = own.astype(F32)
        for n in range(3):
            out = out + got[(n, *where)].astype(F32)
        return out

    def arrived_y():
        for k in range(HK):
            both = pl.ds(2 * k, 2)
            for n in range(3):
                rc(Y1 + 3 * k + n, g_y.at[0, both], r_y1.at[n, both], mate).wait_recv()

    def project(n, _):
        cols = pl.ds(pl.multiple_of(n * 256, 256), 256)
        weight = wf[:, :, :, cols].reshape(2048, 256)
        pro_v[:, cols] = dg(att[...], weight, 1, 0).astype(BF16)
        return 0

    lax.fori_loop(0, 4, project, 0)

    arrived(Z1, r_z1, g_z.at[0])
    for x_ in range(4):
        for y_ in range(4):
            s_z[x_, y_] = total(g_z[z, x_, y_], r_z1, x_, y_).astype(BF16)
    for n in (1, 3, 2):
        send(Z2 + n - 1, s_z.at[turn(x, n)], r_z2.at[n - 1], to_x(n))

    arrived_y()
    for e in range(8):
        for zh_ in range(2):
            value = total(g_y[y, e, zh_], r_y1, e, zh_)
            s_y[zh_ * 2 + e // 4, e % 4] = value.astype(BF16)
    for n in (1, 3, 2):
        send(Y2 + n - 1, s_y.at[turn(z, n)], r_y2.at[n - 1], to_z(n))

    arrived(X1, r_x1, g_x.at[0])
    for zl_ in range(2):
        for sub in range(8):
            value = total(g_x[x, zl_, sub], r_x1, zl_, sub)
            s_x[sub % 4, sub // 4 * 2 + zl_] = value.astype(BF16)
    for n in (1, 3, 2):
        send(X2 + n - 1, s_x.at[turn(y, n)], r_x2.at[n - 1], to_y(n))

    lax.fori_loop(4, 8, project, 0)
    outs = [
        pltpu.make_async_copy(pro_v, pro_hbm, osem.at[0]),
        pltpu.make_async_copy(gq_v, gq_hbm, osem.at[1]),
    ]
    for out in outs:
        out.start()

    arrived(Z2, r_z2, s_z.at[0])
    for y_ in range(4):
        s_z2[y_] = total(s_z[x, y_], r_z2, y_).astype(BF16)
    for n in (1, 3, 2):
        send(Z3 + n - 1, s_z2.at[turn(y, n)], r_z3.at[n - 1], to_y(n))
    arrived(Y2, r_y2, s_y.at[0])
    for x_ in range(4):
        s_y2[x_] = total(s_y[z, x_], r_y2, x_).astype(BF16)
    for n in (1, 3, 2):
        send(Y3 + n - 1, s_y2.at[turn(x, n)], r_y3.at[n - 1], to_x(n))
    arrived(X2, r_x2, s_x.at[0])
    for z_ in range(4):
        s_x2[z_] = total(s_x[y, z_], r_x2, z_).astype(BF16)
    for n in (1, 3, 2):
        send(X3 + n - 1, s_x2.at[turn(z, n)], r_x3.at[n - 1], to_z(n))

    factor = 1.0 / math.sqrt(TOTAL)
    piece_of = zh * 4 + y

    def gather(chunk):
        piece = agb.at[chunk, c, piece_of]
        for n in range(7):
            send(AG + 7 * chunk + n, piece, piece, to_y(n + 1) if n < 3 else to_o(n - 3))

    def origin(n):
        return zh * 4 + turn(y, 3 - n) if n < 3 else (1 - zh) * 4 + turn(y, 7 - n)

    def gathered(chunk):
        for n in range(7):
            piece = agb.at[chunk, c, origin(n)]
            rc(AG + 7 * chunk + n, piece, piece, mate).wait_recv()
        send(AGC + chunk, agb.at[chunk, c], agb.at[chunk, c], mate)

    def finished(chunk):
        half = agb.at[chunk, 1 - c]
        rc(AGC + chunk, half, half, mate).wait_recv()
        outs.append(pltpu.make_async_copy(agb.at[chunk], gw_hbm.at[chunk], osem.at[4 + chunk]))
        outs[-1].start()

    arrived(Y3, r_y3, s_y2.at[0])
    agb[0, c, piece_of] = (total(s_y2[x], r_y3) * factor).astype(BF16)
    gather(0)
    arrived(Z3, r_z3, s_z2.at[0])
    agb[1, c, piece_of, :, 384:512] = (total(s_z2[y], r_z3) * factor).astype(BF16)
    arrived(X3, r_x3, s_x2.at[0])
    agb[1, c, piece_of, :, 0:384] = (total(s_x2[z], r_x3) * factor).astype(BF16)
    gather(1)

    rc(BACK, back_s.at[0], back_r.at[0], before).wait_recv()
    rc(BACK + 1, back_s.at[1], back_r.at[1], before).wait_recv()
    gkv_v[0] = (gk_t[:, TOK : 2 * TOK].T * SCALE + back_r[0].astype(F32)).astype(BF16)
    gkv_v[1] = (gv_t[:, TOK : 2 * TOK].T + back_r[1].astype(F32)).astype(BF16)
    for n, out in enumerate((gk_hbm, gv_hbm)):
        outs.append(pltpu.make_async_copy(gkv_v.at[n], out, osem.at[2 + n]))
        outs[-1].start()

    gathered(0)
    gathered(1)
    finished(0)
    finished(1)
    for copy in sent:
        copy.wait_send()
    for out in outs:
        out.wait()


def finish(pro, gq, gk, gv, gw, pro_o, gq_o, gk_o, gv_o, gw_o, wide, sem):
    pairs = ((pro, pro_o), (gq, gq_o), (gk, gk_o), (gv, gv_o))
    copies = [pltpu.make_async_copy(a, b, sem.at[n]) for n, (a, b) in enumerate(pairs)]
    for copy in copies:
        copy.start()
    for chunk in range(2):
        for half in range(2):
            at = half * 1024 + chunk * 512
            wide[:, at : at + 512] = gw[chunk, half].reshape(TOK, 512).astype(F32)
    copies.append(pltpu.make_async_copy(wide, gw_o, sem.at[4]))
    copies[4].start()
    for copy in copies:
        copy.wait()


def body(queries, key_heads, value_heads, doc_lengths, out_weight, cotangent):
    anywhere = pl.BlockSpec(memory_space=pl.ANY)
    shapes = [
        ((TOK, 2048), BF16),
        ((TOK, 2048), BF16),
        ((2, 512, 512), BF16),
        ((8, 2, 128, 2048), BF16),
        ((TOK, 1024), BF16),
        ((TOK, 2048), BF16),
        ((TOK, 2048), BF16),
        ((HQ, TOK, 512), BF16),
        ((TOK, 512), F32),
        ((4, 8, 2, 32, 512), BF16),
        ((3, 8, 2, 32, 512), BF16),
        ((4, 4, 32, 512), BF16),
        ((3, 4, 32, 512), BF16),
        ((4, 32, 512), BF16),
        ((3, 32, 512), BF16),
        ((4, 2, 8, 32, 384), BF16),
        ((3, 2, 8, 32, 384), BF16),
        ((4, 4, 32, 384), BF16),
        ((3, 4, 32, 384), BF16),
        ((4, 32, 384), BF16),
        ((3, 32, 384), BF16),
        ((4, 4, 4, 32, 128), BF16),
        ((3, 4, 4, 32, 128), BF16),
        ((4, 4, 32, 128), BF16),
        ((3, 4, 32, 128), BF16),
        ((4, 32, 128), BF16),
        ((3, 32, 128), BF16),
        ((2, 2, 8, 32, 512), BF16),
        ((512, 512), F32),
        ((512, 512), F32),
        ((2, TOK, 512), BF16),
        ((2, TOK, 512), BF16),
        ((TOK, 2048), BF16),
        ((TOK, 2048), BF16),
        ((2, TOK, 512), BF16),
    ]
    scratch = [pltpu.VMEM(shape, dtype) for shape, dtype in shapes]
    scratch += [pltpu.SemaphoreType.DMA((n,)) for n in (COPIES, COPIES, 5, 6)]
    results = [
        jax.ShapeDtypeStruct((TOK, 2048), BF16),
        jax.ShapeDtypeStruct((TOK, 2048), BF16),
        jax.ShapeDtypeStruct((TOK, 512), BF16),
        jax.ShapeDtypeStruct((TOK, 512), BF16),
    ]
    outs = pl.pallas_call(
        kernel,
        out_shape=[*results, jax.ShapeDtypeStruct((2, 2, 8, 32, 512), BF16)],
        in_specs=[pl.BlockSpec(memory_space=pltpu.SMEM)] + [anywhere] * 5,
        out_specs=[anywhere] * 5,
        scratch_shapes=scratch,
        compiler_params=pltpu.CompilerParams(
            collective_id=0, has_side_effects=True, vmem_limit_bytes=56 << 20
        ),
        cost_estimate=pl.CostEstimate(
            flops=10_000_000_000, bytes_accessed=12_000_000, transcendentals=2_000_000
        ),
    )(
        doc_lengths,
        queries[0],
        key_heads[0],
        value_heads[0],
        out_weight.reshape(2, 128, DM),
        cotangent[0],
    )
    outs = pl.pallas_call(
        finish,
        out_shape=[*results, jax.ShapeDtypeStruct((TOK, 2048), F32)],
        in_specs=[pl.BlockSpec(memory_space=pltpu.VMEM)] * 5,
        out_specs=[anywhere] * 5,
        scratch_shapes=[pltpu.VMEM((TOK, 2048), F32), pltpu.SemaphoreType.DMA((5,))],
    )(*outs)
    return (*(out[None] for out in outs[:4]), outs[4])


def solution(mesh):
    tokens = P("dp", "seq", None)
    rows = P("dp", None)
    return jax.shard_map(
        body,
        mesh=mesh,
        in_specs=(tokens, tokens, tokens, rows, rows, tokens),
        out_specs=(tokens, tokens, tokens, tokens, rows),
        check_vma=False,
    )
```

time: 89.6 us -> 79.2 us (0.88)
  local copies, waits for them, and re-layouts: 6.13 us -> 0 us
  Pallas kernels: 82.6 us -> 78.3 us
    unnamed x13 -> x0, local copies, waits for them, and re-layouts: 6.13 us -> none
    pallas_call x1 -> x2, Pallas kernels: 82.6 us -> 78.3 us  [the longest x1 74.1 us: body(): pl.pallas_call(kernel, out_shape=[*results, jax.ShapeDtypeStruct((2, 2, 8...]
where the time goes in v2:
time: 79.2 us; the launch traced here: 79.1 us
  Pallas kernels  78.3 us (99%)
  between operations  0.8 us (1%)
    pallas_call x1, Pallas kernels, body(): pl.pallas_call(kernel, out_shape=[*results, jax.ShapeDtypeStruct((2, 2, 8...  74.1 us
    pallas_call x1, Pallas kernels, body(): pl.pallas_call(finish, out_shape=[*results, jax.ShapeDtypeStruct((TOK, 20...  4.24 us

profile of v2, /device:TPU:1, one launch (start us, length us, event | category | flops | bytes accessed | tf_op | source)
XLA Modules:
  0.0 79.1 jit_solution(18143659477457081087)
XLA Ops:
  0.6 74.1 %shard_map.101 = (bf16[256,2048]{1,0:T(8,128)(2,1)}, bf16[256,2048]{1,0:T(8,128)(2,1)}, bf16[256,512]{1,0:T(8,128)(2,1)}, bf16[256,512]{1,0:T(8,128)(2,1)}, bf16[2,2,8,32,512]{4,3,2,1,0:T(8,128)(2,1)}) custom-call(s32[1,32]{1,0:T(1,128)} %len_ref.1, bf16[256,2048]{1,0:T(8,128)(2,1)} %bitcast.9, bf16[256,512]{1,0:T(8,128)(2,1)} %bitcast.14, ...), custom_call_target="tpu_custom_call" | custom-call | flops 10000000000 | bytes 12000000 | tf_op jit(solution)/shard_map/pallas_call | solution.py:478
  74.7 4.2 %shard_map.102 = (bf16[256,2048]{1,0:T(8,128)(2,1)}, bf16[256,2048]{1,0:T(8,128)(2,1)}, bf16[256,512]{1,0:T(8,128)(2,1)}, bf16[256,512]{1,0:T(8,128)(2,1)}, f32[256,2048]{1,0:T(8,128)}) custom-call(bf16[256,2048]{1,0:T(8,128)(2,1)} %get-tuple-element.15.pro, bf16[256,2048]{1,0:T(8,128)(2,1)} %get-tuple-element.16.gq, bf16[256,512]{1,0:T(8,128)(2,1)} %get-tuple-element.17.gk, ...), custom_call_target="tpu_custom_call" | custom-call | tf_op jit(solution)/shard_map/pallas_call | solution.py:498

commit v3 on v2

--- a/solution.py
+++ b/solution.py
@@ -26,9 +26,9 @@
 COT = WC + 7
 ATT = COT + 1
 Y1 = ATT + 4
-X1 = Y1 + 12
-Z1 = X1 + 3
-Y2 = Z1 + 3
+X1 = Y1 + 24
+Z1 = X1 + 6
+Y2 = Z1 + 6
 X2 = Y2 + 3
 Z2 = X2 + 3
 Y3 = Z2 + 3
@@ -193,6 +193,38 @@
     for load in loads[:3]:
         load.wait()
 
+    class Ring:
+        def __init__(self, base, v, to, piece, slot):
+            self.base, self.v, self.piece, self.slot = base, v, piece, slot
+            self.up, self.down = to(1), to(3)
+
+        def start(self):
+            v, piece, slot = self.v, self.piece, self.slot
+            send(self.base, piece(turn(v, 2), 0), slot(0), self.up)
+            send(self.base + 1, piece(turn(v, 2), 1), slot(1), self.down)
+            send(self.base + 2, piece(turn(v, 1), 1), slot(2), self.up)
+            send(self.base + 3, piece(turn(v, 3), 0), slot(3), self.down)
+
+        def relay(self):
+            for part, n, to in ((0, 1, self.up), (1, 3, self.down)):
+                mid, got = self.piece(turn(self.v, n), part), self.slot(part)
+                rc(self.base + part, got, got, mate).wait_recv()
+                mid[...] = (mid[...].astype(F32) + got[...].astype(F32)).astype(BF16)
+                send(self.base + 4 + part, mid, self.slot(4 + part), to)
+
+        def wait(self):
+            for n in range(2, 6):
+                rc(self.base + n, self.slot(n), self.slot(n), mate).wait_recv()
+
+    def ring_of_y(k):
+        return Ring(
+            Y1 + 6 * k, y, to_y, lambda to, part: g_y.at[to, 2 * k + part], lambda n: r_y1.at[n, k]
+        )
+
+    ring_y = [ring_of_y(k) for k in range(HK)]
+    ring_x = Ring(X1, x, to_x, lambda to, part: g_x.at[to, part], lambda n: r_x1.at[n])
+    ring_z = Ring(Z1, z, to_z, lambda to, part: g_z.at[to, part], lambda n: r_z1.at[n])
+
     def head(h):
         return pl.ds(pl.multiple_of(h * DH, DH), DH)
 
@@ -210,7 +242,7 @@
             att[:, head(h)] = dg(p, values, 1, 0).astype(BF16)
             return 0
 
-        lax.fori_loop(0, 4, one, 0)
+        lax.fori_loop(0, 4, one, 0, unroll=True)
         cols = pl.ds(k * 512, 512)
         send(ATT + k, att.at[:, cols], attm.at[:, cols], mate)
 
@@ -235,25 +267,27 @@
                         g_x[e % 4, e // 4, sub, :, 0:256] = rows
                     else:
                         g_x[e % 4, e // 4, sub, :, 256:384] = rows[:, 0:128]
-                        g_z[sub // 4 * 2 + e // 4, e % 4, sub % 4] = rows[:, 128:256]
-        both = pl.ds(2 * k, 2)
-        for n in (1, 3, 2):
-            send(Y1 + 3 * k + n - 1, g_y.at[turn(y, n), both], r_y1.at[n - 1, both], to_y(n))
-
+                        g_z[sub // 4 * 2 + e // 4, e % 4 // 2, e % 2, sub % 4] = rows[:, 128:256]
     fwd(0)
     fwd(1)
     grad_w(0)
+    ring_y[0].start()
+    fwd(2)
     forward_x(0)
-    fwd(2)
     grad_w(1)
-    forward_x(1)
+    ring_y[1].start()
+    ring_y[0].relay()
     fwd(3)
     grad_w(2)
-    forward_x(2)
+    ring_y[2].start()
+    ring_y[1].relay()
+    forward_x(1)
     grad_w(3)
-    for n in (1, 3, 2):
-        send(X1 + n - 1, g_x.at[turn(x, n)], r_x1.at[n - 1], to_x(n))
-        send(Z1 + n - 1, g_z.at[turn(z, n)], r_z1.at[n - 1], to_z(n))
+    ring_y[3].start()
+    ring_x.start()
+    ring_z.start()
+    ring_y[2].relay()
+    forward_z(0)
     loads[4].wait()
 
     def bwd(e):
@@ -273,24 +307,15 @@
             gk_t[head(k), :] += dg(q_v[:, head(h)], grad_s, 0, 0)
             gv_t[head(k), :] += dg(grad_h, p, 0, 0)
 
-    bwd(d)
-    for i in range(1, 4):
+    def bwd_x(i):
         e = shard_x(i, zl)
-        if i == 1:
-            forward_z(0)
         from_mate(i - 1, e)
         bwd(e)
-    for i in range(4):
+
+    def bwd_z(i):
         e = shard_x(i, 1 - zl)
-        if i < 3:
-            forward_z(i + 1)
         from_mate(3 + i, e)
         bwd(e)
-
-    back_s[0] = (gk_t[:, 0:TOK].T * SCALE).astype(BF16)
-    back_s[1] = gv_t[:, 0:TOK].T.astype(BF16)
-    send(BACK, back_s.at[0], back_r.at[0], before)
-    send(BACK + 1, back_s.at[1], back_r.at[1], before)
 
     def arrived(base, dst, source):
         for n in range(3):
@@ -302,44 +327,88 @@
             out = out + got[(n, *where)].astype(F32)
         return out
 
-    def arrived_y():
-        for k in range(HK):
-            both = pl.ds(2 * k, 2)
-            for n in range(3):
-                rc(Y1 + 3 * k + n, g_y.at[0, both], r_y1.at[n, both], mate).wait_recv()
+    def settled(own, got, part, *where):
+        one, two = ((3, 4), (2, 5))[part]
+        return own.astype(F32) + got[(one, *where)].astype(F32) + got[(two, *where)].astype(F32)
 
     def project(n, _):
-        cols = pl.ds(pl.multiple_of(n * 256, 256), 256)
+        cols = pl.ds(n * 256, 256)
         weight = wf[:, :, :, cols].reshape(2048, 256)
         pro_v[:, cols] = dg(att[...], weight, 1, 0).astype(BF16)
         return 0
 
-    lax.fori_loop(0, 4, project, 0)
-
-    arrived(Z1, r_z1, g_z.at[0])
+    def sum_z():
+        ring_z.wait()
+        for x_ in range(4):
+            for y_ in range(4):
+                where = (x_ % 2, y_)
+                value = settled(g_z[(z, x_ // 2, *where)], r_z1, x_ // 2, *where)
+                s_z[x_, y_] = value.astype(BF16)
+        for n in (1, 3, 2):
+            send(Z2 + n - 1, s_z.at[turn(x, n)], r_z2.at[n - 1], to_x(n))
+
+    def sum_y():
+        for ring in ring_y:
+            ring.wait()
+        for e in range(8):
+            for zh_ in range(2):
+                value = settled(g_y[y, e, zh_], r_y1, e % 2, e // 2, zh_)
+                s_y[zh_ * 2 + e // 4, e % 4] = value.astype(BF16)
+        for n in (1, 3, 2):
+            send(Y2 + n - 1, s_y.at[turn(z, n)], r_y2.at[n - 1], to_z(n))
+
+    def sum_x():
+        ring_x.wait()
+        for zl_ in range(2):
+            for sub in range(8):
+                value = settled(g_x[x, zl_, sub], r_x1, zl_, sub)
+                s_x[sub % 4, sub // 4 * 2 + zl_] = value.astype(BF16)
+        for n in (1, 3, 2):
+            send(X2 + n - 1, s_x.at[turn(y, n)], r_x2.at[n - 1], to_y(n))
+
+    bwd(d)
+    forward_x(2)
+    bwd_x(1)
+    bwd_x(2)
+    ring_y[3].relay()
+    forward_z(1)
+    bwd_z(0)
+    forward_z(2)
+    bwd_x(3)
+    ring_x.relay()
+    ring_z.relay()
+    bwd_z(1)
+    sum_y()
+    bwd_z(2)
+    forward_z(3)
+    sum_z()
+    sum_x()
+    bwd_z(3)
+
+    back_s[0] = (gk_t[:, 0:TOK].T * SCALE).astype(BF16)
+    back_s[1] = gv_t[:, 0:TOK].T.astype(BF16)
+    send(BACK, back_s.at[0], back_r.at[0], before)
+    send(BACK + 1, back_s.at[1], back_r.at[1], before)
+
+    for n in range(6):
+        project(n, 0)
+    arrived(Y2, r_y2, s_y.at[0])
     for x_ in range(4):
-        for y_ in range(4):
-            s_z[x_, y_] = total(g_z[z, x_, y_], r_z1, x_, y_).astype(BF16)
+        s_y2[x_] = total(s_y[z, x_], r_y2, x_).astype(BF16)
     for n in (1, 3, 2):
-        send(Z2 + n - 1, s_z.at[turn(x, n)], r_z2.at[n - 1], to_x(n))
-
-    arrived_y()
-    for e in range(8):
-        for zh_ in range(2):
-            value = total(g_y[y, e, zh_], r_y1, e, zh_)
-            s_y[zh_ * 2 + e // 4, e % 4] = value.astype(BF16)
+        send(Y3 + n - 1, s_y2.at[turn(x, n)], r_y3.at[n - 1], to_x(n))
+    arrived(Z2, r_z2, s_z.at[0])
+    for y_ in range(4):
+        s_z2[y_] = total(s_z[x, y_], r_z2, y_).astype(BF16)
     for n in (1, 3, 2):
-        send(Y2 + n - 1, s_y.at[turn(z, n)], r_y2.at[n - 1], to_z(n))
-
-    arrived(X1, r_x1, g_x.at[0])
-    for zl_ in range(2):
-        for sub in range(8):
-            value = total(g_x[x, zl_, sub], r_x1, zl_, sub)
-            s_x[sub % 4, sub // 4 * 2 + zl_] = value.astype(BF16)
+        send(Z3 + n - 1, s_z2.at[turn(y, n)], r_z3.at[n - 1], to_y(n))
+    arrived(X2, r_x2, s_x.at[0])
+    for z_ in range(4):
+        s_x2[z_] = total(s_x[y, z_], r_x2, z_).astype(BF16)
     for n in (1, 3, 2):
-        send(X2 + n - 1, s_x.at[turn(y, n)], r_x2.at[n - 1], to_y(n))
-
-    lax.fori_loop(4, 8, project, 0)
+        send(X3 + n - 1, s_x2.at[turn(z, n)], r_x3.at[n - 1], to_z(n))
+    for n in range(6, 8):
+        project(n, 0)
     outs = [
         pltpu.make_async_copy(pro_v, pro_hbm, osem.at[0]),
         pltpu.make_async_copy(gq_v, gq_hbm, osem.at[1]),
@@ -347,21 +416,6 @@
     for out in outs:
         out.start()
 
-    arrived(Z2, r_z2, s_z.at[0])
-    for y_ in range(4):
-        s_z2[y_] = total(s_z[x, y_], r_z2, y_).astype(BF16)
-    for n in (1, 3, 2):
-        send(Z3 + n - 1, s_z2.at[turn(y, n)], r_z3.at[n - 1], to_y(n))
-    arrived(Y2, r_y2, s_y.at[0])
-    for x_ in range(4):
-        s_y2[x_] = total(s_y[z, x_], r_y2, x_).astype(BF16)
-    for n in (1, 3, 2):
-        send(Y3 + n - 1, s_y2.at[turn(x, n)], r_y3.at[n - 1], to_x(n))
-    arrived(X2, r_x2, s_x.at[0])
-    for z_ in range(4):
-        s_x2[z_] = total(s_x[y, z_], r_x2, z_).astype(BF16)
-    for n in (1, 3, 2):
-        send(X3 + n - 1, s_x2.at[turn(z, n)], r_x3.at[n - 1], to_z(n))
 
     factor = 1.0 / math.sqrt(TOTAL)
     piece_of = zh * 4 + y
@@ -441,19 +495,19 @@
         ((HQ, TOK, 512), BF16),
         ((TOK, 512), F32),
         ((4, 8, 2, 32, 512), BF16),
-        ((3, 8, 2, 32, 512), BF16),
+        ((6, 4, 2, 32, 512), BF16),
         ((4, 4, 32, 512), BF16),
         ((3, 4, 32, 512), BF16),
         ((4, 32, 512), BF16),
         ((3, 32, 512), BF16),
         ((4, 2, 8, 32, 384), BF16),
-        ((3, 2, 8, 32, 384), BF16),
+        ((6, 8, 32, 384), BF16),
         ((4, 4, 32, 384), BF16),
         ((3, 4, 32, 384), BF16),
         ((4, 32, 384), BF16),
         ((3, 32, 384), BF16),
-        ((4, 4, 4, 32, 128), BF16),
-        ((3, 4, 4, 32, 128), BF16),
+        ((4, 2, 2, 4, 32, 128), BF16),
+        ((6, 2, 4, 32, 128), BF16),
         ((4, 4, 32, 128), BF16),
         ((3, 4, 32, 128), BF16),
         ((4, 32, 128), BF16),

time: 79.2 us -> 74.4 us (0.939)
  Pallas kernels: 78.3 us -> 73.4 us
    pallas_call x1, Pallas kernels: 74.1 us -> 69.2 us  [body(): pl.pallas_call(kernel, out_shape=[*results, jax.ShapeDtypeStruct((2, 2, 8...]
where the time goes in v3:
time: 74.4 us; the launch traced here: 74.2 us
  Pallas kernels  73.4 us (99%)
  between operations  0.8 us (1%)
    pallas_call x1, Pallas kernels, body(): pl.pallas_call(kernel, out_shape=[*results, jax.ShapeDtypeStruct((2, 2, 8...  69.2 us
    pallas_call x1, Pallas kernels, body(): pl.pallas_call(finish, out_shape=[*results, jax.ShapeDtypeStruct((TOK, 20...  4.24 us

profile of v3, /device:TPU:1, one launch (start us, length us, event | category | flops | bytes accessed | tf_op | source)
XLA Modules:
  0.0 74.2 jit_solution(8911529185357984681)
XLA Ops:
  0.6 69.2 %shard_map.101 = (bf16[256,2048]{1,0:T(8,128)(2,1)}, bf16[256,2048]{1,0:T(8,128)(2,1)}, bf16[256,512]{1,0:T(8,128)(2,1)}, bf16[256,512]{1,0:T(8,128)(2,1)}, bf16[2,2,8,32,512]{4,3,2,1,0:T(8,128)(2,1)}) custom-call(s32[1,32]{1,0:T(1,128)} %len_ref.1, bf16[256,2048]{1,0:T(8,128)(2,1)} %bitcast.9, bf16[256,512]{1,0:T(8,128)(2,1)} %bitcast.14, ...), custom_call_target="tpu_custom_call" | custom-call | flops 10000000000 | bytes 12000000 | tf_op jit(solution)/shard_map/pallas_call | solution.py:532
  69.8 4.2 %shard_map.102 = (bf16[256,2048]{1,0:T(8,128)(2,1)}, bf16[256,2048]{1,0:T(8,128)(2,1)}, bf16[256,512]{1,0:T(8,128)(2,1)}, bf16[256,512]{1,0:T(8,128)(2,1)}, f32[256,2048]{1,0:T(8,128)}) custom-call(bf16[256,2048]{1,0:T(8,128)(2,1)} %get-tuple-element.15.pro, bf16[256,2048]{1,0:T(8,128)(2,1)} %get-tuple-element.16.gq, bf16[256,512]{1,0:T(8,128)(2,1)} %get-tuple-element.17.gk, ...), custom_call_target="tpu_custom_call" | custom-call | tf_op jit(solution)/shard_map/pallas_call | solution.py:552

commit v4 on v3

--- a/solution.py
+++ b/solution.py
@@ -35,9 +35,9 @@
 X3 = Y3 + 3
 Z3 = X3 + 3
 BACK = Z3 + 3
-AG = BACK + 2
+AG = BACK + 4
 AGC = AG + 14
-COPIES = AGC + 2
+COPIES = AGC + 4
 
 
 def dg(a, b, ca, cb):
@@ -366,6 +366,13 @@
         for n in (1, 3, 2):
             send(X2 + n - 1, s_x.at[turn(y, n)], r_x2.at[n - 1], to_y(n))
 
+    def give_back(part):
+        heads = pl.ds(pl.multiple_of((zl if part == 0 else 1 - zl) * 256, 256), 256)
+        back_s[0, :, heads] = (gk_t[heads, 0:TOK].T * SCALE).astype(BF16)
+        back_s[1, :, heads] = gv_t[heads, 0:TOK].T.astype(BF16)
+        for n in range(2):
+            send(BACK + 2 * part + n, back_s.at[n, :, heads], back_r.at[n, :, heads], before)
+
     bwd(d)
     forward_x(2)
     bwd_x(1)
@@ -375,6 +382,7 @@
     bwd_z(0)
     forward_z(2)
     bwd_x(3)
+    give_back(0)
     ring_x.relay()
     ring_z.relay()
     bwd_z(1)
@@ -384,11 +392,7 @@
     sum_z()
     sum_x()
     bwd_z(3)
-
-    back_s[0] = (gk_t[:, 0:TOK].T * SCALE).astype(BF16)
-    back_s[1] = gv_t[:, 0:TOK].T.astype(BF16)
-    send(BACK, back_s.at[0], back_r.at[0], before)
-    send(BACK + 1, back_s.at[1], back_r.at[1], before)
+    give_back(1)
 
     for n in range(6):
         project(n, 0)
@@ -428,15 +432,18 @@
     def origin(n):
         return zh * 4 + turn(y, 3 - n) if n < 3 else (1 - zh) * 4 + turn(y, 7 - n)
 
-    def gathered(chunk):
-        for n in range(7):
+    def gathered(chunk, part):
+        for n in (range(3), range(3, 7))[part]:
             piece = agb.at[chunk, c, origin(n)]
             rc(AG + 7 * chunk + n, piece, piece, mate).wait_recv()
-        send(AGC + chunk, agb.at[chunk, c], agb.at[chunk, c], mate)
+        which = zh if part == 0 else 1 - zh
+        half = agb.at[chunk, c, pl.ds(which * 4, 4)]
+        send(AGC + 2 * chunk + part, half, half, mate)
 
     def finished(chunk):
-        half = agb.at[chunk, 1 - c]
-        rc(AGC + chunk, half, half, mate).wait_recv()
+        for part, which in enumerate((zh, 1 - zh)):
+            half = agb.at[chunk, 1 - c, pl.ds(which * 4, 4)]
+            rc(AGC + 2 * chunk + part, half, half, mate).wait_recv()
         outs.append(pltpu.make_async_copy(agb.at[chunk], gw_hbm.at[chunk], osem.at[4 + chunk]))
         outs[-1].start()
 
@@ -449,17 +456,22 @@
     agb[1, c, piece_of, :, 0:384] = (total(s_x2[z], r_x3) * factor).astype(BF16)
     gather(1)
 
-    rc(BACK, back_s.at[0], back_r.at[0], before).wait_recv()
-    rc(BACK + 1, back_s.at[1], back_r.at[1], before).wait_recv()
+    for part in range(2):
+        heads = pl.ds(pl.multiple_of((zl if part == 0 else 1 - zl) * 256, 256), 256)
+        for n in range(2):
+            got = back_r.at[n, :, heads]
+            rc(BACK + 2 * part + n, got, got, before).wait_recv()
     gkv_v[0] = (gk_t[:, TOK : 2 * TOK].T * SCALE + back_r[0].astype(F32)).astype(BF16)
     gkv_v[1] = (gv_t[:, TOK : 2 * TOK].T + back_r[1].astype(F32)).astype(BF16)
     for n, out in enumerate((gk_hbm, gv_hbm)):
         outs.append(pltpu.make_async_copy(gkv_v.at[n], out, osem.at[2 + n]))
         outs[-1].start()
 
-    gathered(0)
-    gathered(1)
+    gathered(0, 0)
+    gathered(1, 0)
+    gathered(0, 1)
     finished(0)
+    gathered(1, 1)
     finished(1)
     for copy in sent:
         copy.wait_send()
@@ -467,18 +479,33 @@
         out.wait()
 
 
-def finish(pro, gq, gk, gv, gw, pro_o, gq_o, gk_o, gv_o, gw_o, wide, sem):
-    pairs = ((pro, pro_o), (gq, gq_o), (gk, gk_o), (gv, gv_o))
-    copies = [pltpu.make_async_copy(a, b, sem.at[n]) for n, (a, b) in enumerate(pairs)]
-    for copy in copies:
+def finish(
+    pro, gq, gk, gv, gw, pro_o, gq_o, gk_o, gv_o, gw_o,
+    pro_v, gq_v, gk_v, gv_v, gw_v, wide, in_sem, out_sem,
+):
+    pieces = [(gw.at[a, b], gw_v.at[a, b], (a, b)) for a in range(2) for b in range(2)]
+    for source, held, out in ((pro, pro_v, pro_o), (gq, gq_v, gq_o)):
+        for n in range(2):
+            rows = pl.ds(n * 128, 128)
+            pieces.append((source.at[rows], held.at[rows], out.at[rows]))
+    pieces += [(gk, gk_v, gk_o), (gv, gv_v, gv_o)]
+    got = [
+        pltpu.make_async_copy(source, held, in_sem.at[n])
+        for n, (source, held, _) in enumerate(pieces)
+    ]
+    for copy in got:
         copy.start()
-    for chunk in range(2):
-        for half in range(2):
-            at = half * 1024 + chunk * 512
-            wide[:, at : at + 512] = gw[chunk, half].reshape(TOK, 512).astype(F32)
-    copies.append(pltpu.make_async_copy(wide, gw_o, sem.at[4]))
-    copies[4].start()
-    for copy in copies:
+    put = []
+    for n, (_, held, out) in enumerate(pieces):
+        got[n].wait()
+        if n < 4:
+            a, b = out
+            cols = pl.ds(b * 1024 + a * 512, 512)
+            wide[:, cols] = gw_v[a, b].reshape(TOK, 512).astype(F32)
+            held, out = wide.at[:, cols], gw_o.at[:, cols]
+        put.append(pltpu.make_async_copy(held, out, out_sem.at[n]))
+        put[n].start()
+    for copy in put:
         copy.wait()
 
 
@@ -552,9 +579,15 @@
     outs = pl.pallas_call(
         finish,
         out_shape=[*results, jax.ShapeDtypeStruct((TOK, 2048), F32)],
-        in_specs=[pl.BlockSpec(memory_space=pltpu.VMEM)] * 5,
+        in_specs=[anywhere] * 5,
         out_specs=[anywhere] * 5,
-        scratch_shapes=[pltpu.VMEM((TOK, 2048), F32), pltpu.SemaphoreType.DMA((5,))],
+        scratch_shapes=[
+            *(pltpu.VMEM(result.shape, BF16) for result in results),
+            pltpu.VMEM((2, 2, 8, 32, 512), BF16),
+            pltpu.VMEM((TOK, 2048), F32),
+            pltpu.SemaphoreType.DMA((10,)),
+            pltpu.SemaphoreType.DMA((10,)),
+        ],
     )(*outs)
     return (*(out[None] for out in outs[:4]), outs[4])
 

time: 74.4 us -> 69.7 us (0.937)
  Pallas kernels: 73.4 us -> 68.8 us
    pallas_call x1, Pallas kernels: 69.2 us -> 65.5 us  [body(): pl.pallas_call(kernel, out_shape=[*results, jax.ShapeDtypeStruct((2, 2, 8...]
    pallas_call x1, Pallas kernels: 4.24 us -> 3.32 us  [body(): pl.pallas_call(finish, out_shape=[*results, jax.ShapeDtypeStruct((TOK, 20...]
where the time goes in v4:
time: 69.7 us; the launch traced here: 69.6 us
  Pallas kernels  68.8 us (99%)
  between operations  0.8 us (1%)
    pallas_call x1, Pallas kernels, body(): pl.pallas_call(kernel, out_shape=[*results, jax.ShapeDtypeStruct((2, 2, 8...  65.5 us
    pallas_call x1, Pallas kernels, body(): pl.pallas_call(finish, out_shape=[*results, jax.ShapeDtypeStruct((TOK, 20...  3.32 us

profile of v4, /device:TPU:1, one launch (start us, length us, event | category | flops | bytes accessed | tf_op | source)
XLA Modules:
  0.0 69.6 jit_solution(82705299180501060)
XLA Ops:
  0.6 65.5 %shard_map.101 = (bf16[256,2048]{1,0:T(8,128)(2,1)}, bf16[256,2048]{1,0:T(8,128)(2,1)}, bf16[256,512]{1,0:T(8,128)(2,1)}, bf16[256,512]{1,0:T(8,128)(2,1)}, bf16[2,2,8,32,512]{4,3,2,1,0:T(8,128)(2,1)}) custom-call(s32[1,32]{1,0:T(1,128)} %len_ref.1, bf16[256,2048]{1,0:T(8,128)(2,1)} %bitcast.9, bf16[256,512]{1,0:T(8,128)(2,1)} %bitcast.14, ...), custom_call_target="tpu_custom_call" | custom-call | flops 10000000000 | bytes 12000000 | tf_op jit(solution)/shard_map/pallas_call | solution.py:559
  66.1 3.3 %shard_map.102 = (bf16[256,2048]{1,0:T(8,128)(2,1)}, bf16[256,2048]{1,0:T(8,128)(2,1)}, bf16[256,512]{1,0:T(8,128)(2,1)}, bf16[256,512]{1,0:T(8,128)(2,1)}, f32[256,2048]{1,0:T(8,128)}) custom-call(bf16[256,2048]{1,0:T(8,128)(2,1)} %get-tuple-element.15.pro, bf16[256,2048]{1,0:T(8,128)(2,1)} %get-tuple-element.16.gq, bf16[256,512]{1,0:T(8,128)(2,1)} %get-tuple-element.17.gk, ...), custom_call_target="tpu_custom_call" | custom-call | tf_op jit(solution)/shard_map/pallas_call | solution.py:579

commit v5 on v4

--- a/solution.py
+++ b/solution.py
@@ -15,6 +15,7 @@
 DOCS = 32
 TOTAL = 32768
 SCALE = 1.0 / math.sqrt(DH)
+LOG2E = math.log2(math.e)
 F32 = jnp.float32
 BF16 = jnp.bfloat16
 MESH = pl.DeviceIdType.MESH
@@ -47,7 +48,7 @@
 def kernel(
     len_ref, q_hbm, k_hbm, v_hbm, w_hbm, cot_hbm,
     pro_hbm, gq_hbm, gk_hbm, gv_hbm, gw_hbm,
-    q_v, cot_v, kv, wf, cotm, att, attm, prob, bias,
+    q_v, cot_v, kv, wf, cotm, att, attm, prob, bias, inverse,
     g_y, r_y1, s_y, r_y2, s_y2, r_y3,
     g_x, r_x1, s_x, r_x2, s_x2, r_x3,
     g_z, r_z1, s_z, r_z2, s_z2, r_z3,
@@ -233,13 +234,17 @@
             rc(*halo(n)).wait_recv()
         keys, values = kv[0, :, head(k)], kv[1, :, head(k)]
 
+        wide = jnp.concatenate([values, jnp.ones_like(values)], axis=1)
+
         def one(g, _):
             h = k * 4 + g
-            scores = dg(q_v[:, head(h)], keys, 1, 1) * SCALE + bias[...]
-            e = jnp.exp(scores - jnp.max(scores, axis=-1, keepdims=True))
-            p = (e * (1.0 / jnp.sum(e, axis=-1, keepdims=True))).astype(BF16)
-            prob[h] = p
-            att[:, head(h)] = dg(p, values, 1, 0).astype(BF16)
+            scores = dg(q_v[:, head(h)], keys, 1, 1) * (SCALE * LOG2E) + bias[...]
+            e = jnp.exp2(scores - jnp.max(scores, axis=-1, keepdims=True)).astype(BF16)
+            prob[h] = e
+            out = dg(e, wide, 1, 0)
+            inv = 1.0 / out[:, DH:]
+            inverse[:, head(h)] = inv
+            att[:, head(h)] = (out[:, :DH] * inv).astype(BF16)
             return 0
 
         lax.fori_loop(0, 4, one, 0, unroll=True)
@@ -272,8 +277,8 @@
     fwd(1)
     grad_w(0)
     ring_y[0].start()
+    forward_x(0)
     fwd(2)
-    forward_x(0)
     grad_w(1)
     ring_y[1].start()
     ring_y[0].relay()
@@ -302,10 +307,13 @@
                 grad_h.astype(F32) * att[:, head(h)].astype(F32), axis=-1, keepdims=True
             )
             p = prob[h]
-            grad_s = (p.astype(F32) * (dg(grad_h, values, 1, 1) - delta)).astype(BF16)
+            inv = inverse[:, head(h)]
+            grad_n = (grad_h.astype(F32) * inv).astype(BF16)
+            inv = jnp.concatenate([inv] * 4, axis=1)
+            grad_s = (p.astype(F32) * ((dg(grad_h, values, 1, 1) - delta) * inv)).astype(BF16)
             gq_v[:, head(h)] = (dg(grad_s, keys, 1, 0) * SCALE).astype(BF16)
             gk_t[head(k), :] += dg(q_v[:, head(h)], grad_s, 0, 0)
-            gv_t[head(k), :] += dg(grad_h, p, 0, 0)
+            gv_t[head(k), :] += dg(grad_n, p, 0, 0)
 
     def bwd_x(i):
         e = shard_x(i, zl)
@@ -521,6 +529,7 @@
         ((TOK, 2048), BF16),
         ((HQ, TOK, 512), BF16),
         ((TOK, 512), F32),
+        ((TOK, 2048), F32),
         ((4, 8, 2, 32, 512), BF16),
         ((6, 4, 2, 32, 512), BF16),
         ((4, 4, 32, 512), BF16),

time: 69.7 us -> 69.1 us (level)
  Pallas kernels: 68.8 us -> 68.1 us
where the time goes in v5:
time: 69.1 us; the launch traced here: 69 us
  Pallas kernels  68.1 us (99%)
  between operations  0.8 us (1%)
    pallas_call x1, Pallas kernels, body(): pl.pallas_call(kernel, out_shape=[*results, jax.ShapeDtypeStruct((2, 2, 8...  64.8 us
    pallas_call x1, Pallas kernels, body(): pl.pallas_call(finish, out_shape=[*results, jax.ShapeDtypeStruct((TOK, 20...  3.32 us

profile of v5, /device:TPU:1, one launch (start us, length us, event | category | flops | bytes accessed | tf_op | source)
XLA Modules:
  0.0 69.0 jit_solution(91519837697652804)
XLA Ops:
  0.6 64.8 %shard_map.101 = (bf16[256,2048]{1,0:T(8,128)(2,1)}, bf16[256,2048]{1,0:T(8,128)(2,1)}, bf16[256,512]{1,0:T(8,128)(2,1)}, bf16[256,512]{1,0:T(8,128)(2,1)}, bf16[2,2,8,32,512]{4,3,2,1,0:T(8,128)(2,1)}) custom-call(s32[1,32]{1,0:T(1,128)} %len_ref.1, bf16[256,2048]{1,0:T(8,128)(2,1)} %bitcast.9, bf16[256,512]{1,0:T(8,128)(2,1)} %bitcast.14, ...), custom_call_target="tpu_custom_call" | custom-call | flops 10000000000 | bytes 12000000 | tf_op jit(solution)/shard_map/pallas_call | solution.py:568
  65.5 3.3 %shard_map.102 = (bf16[256,2048]{1,0:T(8,128)(2,1)}, bf16[256,2048]{1,0:T(8,128)(2,1)}, bf16[256,512]{1,0:T(8,128)(2,1)}, bf16[256,512]{1,0:T(8,128)(2,1)}, f32[256,2048]{1,0:T(8,128)}) custom-call(bf16[256,2048]{1,0:T(8,128)(2,1)} %get-tuple-element.15.pro, bf16[256,2048]{1,0:T(8,128)(2,1)} %get-tuple-element.16.gq, bf16[256,512]{1,0:T(8,128)(2,1)} %get-tuple-element.17.gk, ...), custom_call_target="tpu_custom_call" | custom-call | tf_op jit(solution)/shard_map/pallas_call | solution.py:588

commit v6 on v5

--- a/solution.py
+++ b/solution.py
@@ -116,7 +116,6 @@
     barrier = pltpu.get_barrier_semaphore()
     peers = [mate, after, before]
     peers += [f(n) for f in (to_x, to_y, to_z) for n in (1, 2, 3)]
-    peers += [to_o(n) for n in (1, 2, 3)]
     for peer in peers:
         pl.semaphore_signal(barrier, inc=1, device_id=peer, device_id_type=MESH)
 

time: 69.1 us -> 72.3 us (1.046)
  Pallas kernels: 68.1 us -> 71.3 us
    pallas_call x1, Pallas kernels: 64.8 us -> 68 us  [body(): pl.pallas_call(kernel, out_shape=[*results, jax.ShapeDtypeStruct((2, 2, 8...]
where the time goes in v6:
time: 72.3 us; the launch traced here: 72.1 us
  Pallas kernels  71.3 us (99%)
  between operations  0.8 us (1%)
    pallas_call x1, Pallas kernels, body(): pl.pallas_call(kernel, out_shape=[*results, jax.ShapeDtypeStruct((2, 2, 8...  68 us
    pallas_call x1, Pallas kernels, body(): pl.pallas_call(finish, out_shape=[*results, jax.ShapeDtypeStruct((TOK, 20...  3.32 us

profile of v6, /device:TPU:1, one launch (start us, length us, event | category | flops | bytes accessed | tf_op | source)
XLA Modules:
  0.0 72.1 jit_solution(1666919247507512107)
XLA Ops:
  0.6 68.0 %shard_map.101 = (bf16[256,2048]{1,0:T(8,128)(2,1)}, bf16[256,2048]{1,0:T(8,128)(2,1)}, bf16[256,512]{1,0:T(8,128)(2,1)}, bf16[256,512]{1,0:T(8,128)(2,1)}, bf16[2,2,8,32,512]{4,3,2,1,0:T(8,128)(2,1)}) custom-call(s32[1,32]{1,0:T(1,128)} %len_ref.1, bf16[256,2048]{1,0:T(8,128)(2,1)} %bitcast.9, bf16[256,512]{1,0:T(8,128)(2,1)} %bitcast.14, ...), custom_call_target="tpu_custom_call" | custom-call | flops 10000000000 | bytes 12000000 | tf_op jit(solution)/shard_map/pallas_call | solution.py:567
  68.6 3.3 %shard_map.102 = (bf16[256,2048]{1,0:T(8,128)(2,1)}, bf16[256,2048]{1,0:T(8,128)(2,1)}, bf16[256,512]{1,0:T(8,128)(2,1)}, bf16[256,512]{1,0:T(8,128)(2,1)}, f32[256,2048]{1,0:T(8,128)}) custom-call(bf16[256,2048]{1,0:T(8,128)(2,1)} %get-tuple-element.15.pro, bf16[256,2048]{1,0:T(8,128)(2,1)} %get-tuple-element.16.gq, bf16[256,512]{1,0:T(8,128)(2,1)} %get-tuple-element.17.gk, ...), custom_call_target="tpu_custom_call" | custom-call | tf_op jit(solution)/shard_map/pallas_call | solution.py:587
